TPU v7x, 32 devices: a whole 2x2x4 slice. The times are simulated.
32 devices in a mesh: grp: 8 (over z, y), row: 4 (over x, core).
Axes of the slice: x: 2, y: 2, z: 4, core: 2. Of those that a mesh axis runs over, the one named last changes fastest.
Arguments:
- hidden_in: bfloat16 [16384, 768], P(('grp', 'row')), may hold values from -6 to 6
- cotangent: bfloat16 [16384, 768], P(('grp', 'row')), may hold values from -6 to 6
- w_qkv: bfloat16 [768, 2304], P('row', 'grp'), may hold values from -0.21875 to 0.21875
- w_out: bfloat16 [768, 768], P('row', 'grp'), may hold values from -0.625 to 0.625
- w_fc: bfloat16 [768, 3072], P('row', 'grp'), may hold values from -0.21875 to 0.21875
- w_proj: bfloat16 [3072, 768], P('row', 'grp'), may hold values from -0.15625 to 0.15625
- vectors: bfloat16 [8, 768], P('row', 'grp')
- fc_bias: bfloat16 [3072], P(('grp', 'row')), may hold values from -1.5 to 1.5
- first_qkv: float32 [768, 2304], P('row', 'grp'), may hold values from -0.18 to 0.18
- first_out: float32 [768, 768], P('row', 'grp'), may hold values from -0.18 to 0.18
- first_fc: float32 [768, 3072], P('row', 'grp'), may hold values from -0.18 to 0.18
- first_proj: float32 [3072, 768], P('row', 'grp'), may hold values from -0.18 to 0.18
- first_vectors: float32 [8, 768], P('row', 'grp'), may hold values from -0.18 to 0.18
- first_fc_bias: float32 [3072], P(('grp', 'row')), may hold values from -0.18 to 0.18
- second_qkv: float32 [768, 2304], P('row', 'grp'), may hold values from 1e-05 to 0.001
- second_out: float32 [768, 768], P('row', 'grp'), may hold values from 1e-05 to 0.001
- second_fc: float32 [768, 3072], P('row', 'grp'), may hold values from 1e-05 to 0.001
- second_proj: float32 [3072, 768], P('row', 'grp'), may hold values from 1e-05 to 0.001
- second_vectors: float32 [8, 768], P('row', 'grp'), may hold values from 1e-05 to 0.001
- second_fc_bias: float32 [3072], P(('grp', 'row')), may hold values from 1e-05 to 0.001
- seg_ends: int32 [32, 8], P(('grp', 'row')), may hold values from 1 to 512, as said below
- pass_counts: int32 [8], P('grp'), may hold values from 1 to 2, as said below
- reset_flag: int32 [768], replicated, may hold values 0 or 1
Outputs:
- hidden: bfloat16 [16384, 768], P(('grp', 'row'))
- input_grad: float32 [16384, 768], P(('grp', 'row'))
- grad_qkv: float32 [768, 2304], P('row', 'grp')
- grad_out: float32 [768, 768], P('row', 'grp')
- grad_fc: float32 [768, 3072], P('row', 'grp')
- grad_proj: float32 [3072, 768], P('row', 'grp')
- grad_vectors: float32 [8, 768], P('row', 'grp')
- grad_fc_bias: float32 [3072], P(('grp', 'row'))
- new_qkv: bfloat16 [768, 2304], P('row', 'grp')
- new_out: bfloat16 [768, 768], P('row', 'grp')
- new_fc: bfloat16 [768, 3072], P('row', 'grp')
- new_proj: bfloat16 [3072, 768], P('row', 'grp')
- new_vectors: bfloat16 [8, 768], P('row', 'grp')
- new_fc_bias: bfloat16 [3072], P(('grp', 'row'))
- new_first_qkv: float32 [768, 2304], P('row', 'grp')
- new_first_out: float32 [768, 768], P('row', 'grp')
- new_first_fc: float32 [768, 3072], P('row', 'grp')
- new_first_proj: float32 [3072, 768], P('row', 'grp')
- new_first_vectors: float32 [8, 768], P('row', 'grp')
- new_first_fc_bias: float32 [3072], P(('grp', 'row'))
- new_second_qkv: float32 [768, 2304], P('row', 'grp')
- new_second_out: float32 [768, 768], P('row', 'grp')
- new_second_fc: float32 [768, 3072], P('row', 'grp')
- new_second_proj: float32 [3072, 768], P('row', 'grp')
- new_second_vectors: float32 [8, 768], P('row', 'grp')
- new_second_fc_bias: float32 [3072], P(('grp', 'row'))
Inputs may be any that keep to these rules, and one draw needn't show every extreme that they name: `seg_ends`: each row's ends never fall; tokens at or after a row's last end are padding, and some row has no padding. `pass_counts`: some group runs 2 passes and some group runs one.
All inputs are finite; a program needn't handle non-finite values.
Results may differ from a plain program's by a relative error of at most 0.02.
Values may be sent and summed in bfloat16 or wider, within the bound.
No kernel may reach another device: no remote copies, remote signals or barrier semaphores. Data moves between devices by JAX's collectives and lax.ppermute only.
A program may use at most 320 MiB of HBM per device.

v0:
```python
import jax
import jax.numpy as jnp
from jax import lax
from jax.sharding import PartitionSpec as P

D = 768
HEADS = 12
HEAD = 64
FF = 3072
PASSES = 2
STEP = 10


LEARN_RATE = 0.03
WEIGHT_DECAY = 0.1


def layer_norm(h, gain, bias):
    mean_h = jnp.mean(h, -1, keepdims=True)
    centred = h - mean_h
    var_h = jnp.mean(centred * centred, -1, keepdims=True)
    return centred * lax.rsqrt(var_h + 1e-05) * gain + bias


def gelu_tanh(value):
    return jax.nn.gelu(value, approximate=True)


def gather_weights(shards):
    rows = (
        lax.all_gather(shards[0], "row", axis=0, tiled=True),
        lax.all_gather(shards[1], "row", axis=0, tiled=True),
        lax.all_gather(shards[2], "row", axis=0, tiled=True),
        lax.all_gather(shards[3], "row", axis=0, tiled=True),
        lax.all_gather(shards[4], "row", axis=0, tiled=True),
        lax.all_gather(shards[5], "row", axis=0, tiled=True),
    )
    return (
        lax.all_gather(rows[0], "grp", axis=1, tiled=True),
        lax.all_gather(rows[1], "grp", axis=1, tiled=True),
        lax.all_gather(rows[2], "grp", axis=1, tiled=True),
        lax.all_gather(rows[3], "grp", axis=1, tiled=True),
        lax.all_gather(rows[4], "grp", axis=1, tiled=True),
        lax.all_gather(rows[5], "grp", axis=0, tiled=True),
    )


def reduce_grp(parts):
    return (
        lax.psum_scatter(parts[0], "grp", scatter_dimension=1, tiled=True),
        lax.psum_scatter(parts[1], "grp", scatter_dimension=1, tiled=True),
        lax.psum_scatter(parts[2], "grp", scatter_dimension=1, tiled=True),
        lax.psum_scatter(parts[3], "grp", scatter_dimension=1, tiled=True),
        lax.psum_scatter(parts[4], "grp", scatter_dimension=1, tiled=True),
        lax.psum_scatter(parts[5], "grp", scatter_dimension=0, tiled=True),
    )


def reduce_row(parts):
    return (
        lax.psum_scatter(parts[0], "row", scatter_dimension=0, tiled=True),
        lax.psum_scatter(parts[1], "row", scatter_dimension=0, tiled=True),
        lax.psum_scatter(parts[2], "row", scatter_dimension=0, tiled=True),
        lax.psum_scatter(parts[3], "row", scatter_dimension=0, tiled=True),
        lax.psum_scatter(parts[4], "row", scatter_dimension=0, tiled=True),
        lax.psum_scatter(parts[5], "row", scatter_dimension=0, tiled=True),
    )


def head_scores(query, keys, visible):
    scores = jnp.einsum("qhd,khd->hqk", query, keys, preferred_element_type=jnp.float32) * HEAD ** (
        -0.5
    )
    return jnp.where(visible[None], scores, -1e30)


def forward_pass(h, full, visible):
    w_qkv, w_out, w_fc, w_proj, vectors, fc_bias = full
    vec = vectors.astype(jnp.float32)
    length = h.shape[0]
    a_low = layer_norm(h, vec[0], vec[1]).astype(jnp.bfloat16)
    qkv = jnp.dot(a_low, w_qkv, preferred_element_type=jnp.float32)
    query = (qkv[:, :D] + vec[2]).astype(jnp.bfloat16).reshape(length, HEADS, HEAD)
    keys = qkv[:, D : 2 * D].astype(jnp.bfloat16).reshape(length, HEADS, HEAD)
    values = (qkv[:, 2 * D :] + vec[3]).astype(jnp.bfloat16).reshape(length, HEADS, HEAD)
    scores = head_scores(query, keys, visible)
    top = jnp.max(scores, -1, keepdims=True)
    expo = jnp.exp(scores - top)
    denom = jnp.sum(expo, -1, keepdims=True)
    probs_low = (expo / denom).astype(jnp.bfloat16)
    log_total = top + jnp.log(denom)
    mixed = jnp.einsum("hqk,khd->qhd", probs_low, values, preferred_element_type=jnp.float32)
    mixed = mixed.reshape(length, D).astype(jnp.bfloat16)
    h_mid = h + jnp.dot(mixed, w_out, preferred_element_type=jnp.float32) + vec[4]
    c_low = layer_norm(h_mid, vec[5], vec[6]).astype(jnp.bfloat16)
    f_pre = jnp.dot(c_low, w_fc, preferred_element_type=jnp.float32) + fc_bias.astype(jnp.float32)
    g_low = gelu_tanh(f_pre).astype(jnp.bfloat16)
    h_out = h_mid + jnp.dot(g_low, w_proj, preferred_element_type=jnp.float32) + vec[7]
    kept = (h, a_low, query, keys, values, log_total, mixed, h_mid, c_low, f_pre, g_low)
    return (h_out, kept)


def empty_kept(length):
    flat = jnp.zeros((length, D), jnp.float32)
    flat_low = jnp.zeros((length, D), jnp.bfloat16)
    split_low = jnp.zeros((length, HEADS, HEAD), jnp.bfloat16)
    return (
        flat,
        flat_low,
        split_low,
        split_low,
        split_low,
        jnp.zeros((HEADS, length, 1), jnp.float32),
        flat_low,
        flat,
        flat_low,
        jnp.zeros((length, FF), jnp.float32),
        jnp.zeros((length, FF), jnp.bfloat16),
    )


def backward_pass(d_out, kept, full, visible):
    w_qkv, w_out, w_fc, w_proj, vectors, fc_bias = full
    h, a_low, query, keys, values, log_total, mixed, h_mid, c_low, f_pre, g_low = kept
    vec = vectors.astype(jnp.float32)
    length = h.shape[0]
    d_out_low = d_out.astype(jnp.bfloat16)
    grad_proj = jnp.dot(g_low.T, d_out_low, preferred_element_type=jnp.float32)
    d_gelu = jnp.dot(d_out_low, w_proj.T, preferred_element_type=jnp.float32)
    d_fpre = jax.vjp(gelu_tanh, f_pre)[1](d_gelu)[0]
    d_fpre_low = d_fpre.astype(jnp.bfloat16)
    grad_fc = jnp.dot(c_low.T, d_fpre_low, preferred_element_type=jnp.float32)
    d_c = jnp.dot(d_fpre_low, w_fc.T, preferred_element_type=jnp.float32)
    norm_back2 = jax.vjp(layer_norm, h_mid, vec[5], vec[6])[1]
    d_mid_norm, d_gain2, d_bias2 = norm_back2(d_c)
    d_mid = d_out + d_mid_norm
    d_mid_low = d_mid.astype(jnp.bfloat16)
    grad_out = jnp.dot(mixed.T, d_mid_low, preferred_element_type=jnp.float32)
    d_mixed = jnp.dot(d_mid_low, w_out.T, preferred_element_type=jnp.float32)
    d_mixed = d_mixed.astype(jnp.bfloat16).reshape(length, HEADS, HEAD)
    probs = jnp.exp(head_scores(query, keys, visible) - log_total)
    probs_low = probs.astype(jnp.bfloat16)
    d_values = jnp.einsum("hqk,qhd->khd", probs_low, d_mixed, preferred_element_type=jnp.float32)
    d_probs = jnp.einsum("qhd,khd->hqk", d_mixed, values, preferred_element_type=jnp.float32)
    d_scores = probs * (d_probs - jnp.sum(probs * d_probs, -1, keepdims=True))
    d_scores_low = (d_scores * HEAD ** (-0.5)).astype(jnp.bfloat16)
    d_query = jnp.einsum(
        "hqk,khd->qhd", d_scores_low, keys, preferred_element_type=jnp.float32
    ).reshape(length, D)
    d_keys = jnp.einsum(
        "hqk,qhd->khd", d_scores_low, query, preferred_element_type=jnp.float32
    ).reshape(length, D)
    d_values = d_values.reshape(length, D)
    d_qkv_low = jnp.concatenate([d_query, d_keys, d_values], 1).astype(jnp.bfloat16)
    grad_qkv = jnp.dot(a_low.T, d_qkv_low, preferred_element_type=jnp.float32)
    d_a = jnp.dot(d_qkv_low, w_qkv.T, preferred_element_type=jnp.float32)
    norm_back1 = jax.vjp(layer_norm, h, vec[0], vec[1])[1]
    d_in_norm, d_gain1, d_bias1 = norm_back1(d_a)
    d_in = d_mid + d_in_norm
    grad_vectors = jnp.stack(
        [
            d_gain1,
            d_bias1,
            jnp.sum(d_query, 0),
            jnp.sum(d_values, 0),
            jnp.sum(d_mid, 0),
            d_gain2,
            d_bias2,
            jnp.sum(d_out, 0),
        ]
    )
    grad_fc_bias = jnp.sum(d_fpre, 0)
    return (d_in, (grad_qkv, grad_out, grad_fc, grad_proj, grad_vectors, grad_fc_bias))


def adam_update(weight, first, second, grad, keep_frac, t_step):
    first_new = 0.9 * first * keep_frac + 0.1 * grad
    second_new = 0.95 * second * keep_frac + 0.05 * grad * grad
    first_hat = first_new / (1.0 - 0.9**t_step)
    second_hat = second_new / (1.0 - 0.95**t_step)
    weight_new = weight.astype(jnp.float32) * (
        1.0 - LEARN_RATE * WEIGHT_DECAY
    ) - LEARN_RATE * first_hat / (jnp.sqrt(second_hat) + 1e-08)
    return (weight_new.astype(jnp.bfloat16), first_new, second_new)


def body(
    hidden_in,
    cotangent,
    w_qkv,
    w_out,
    w_fc,
    w_proj,
    vectors,
    fc_bias,
    first_qkv,
    first_out,
    first_fc,
    first_proj,
    first_vectors,
    first_fc_bias,
    second_qkv,
    second_out,
    second_fc,
    second_proj,
    second_vectors,
    second_fc_bias,
    seg_ends,
    pass_counts,
    reset_flag,
):
    length = hidden_in.shape[0]
    position = jnp.arange(length, dtype=jnp.int32)
    ends = seg_ends[0]
    segment = jnp.sum((position[:, None] >= ends[None, :]).astype(jnp.int32), 1)
    valid = position < ends[-1]
    visible = (segment[:, None] == segment[None, :]) & (position[None, :] <= position[:, None])
    total = lax.psum(jnp.sum(valid.astype(jnp.float32)), ("grp", "row"))
    passes_here = pass_counts[0]
    shards = (w_qkv, w_out, w_fc, w_proj, vectors, fc_bias)
    state = hidden_in.astype(jnp.float32)
    kept_all = []
    for turn in range(PASSES):
        full = gather_weights(shards)

        def run_fwd(h, full=full):
            return forward_pass(h, full, visible)

        def skip_fwd(h):
            return (h, empty_kept(length))

        state, kept = lax.cond(turn < passes_here, run_fwd, skip_fwd, state)
        kept_all.append(kept)
    hidden = state.astype(jnp.bfloat16)
    grads = (
        jnp.zeros((D, 3 * D), jnp.float32),
        jnp.zeros((D, D), jnp.float32),
        jnp.zeros((D, FF), jnp.float32),
        jnp.zeros((FF, D), jnp.float32),
        jnp.zeros((8, D), jnp.float32),
        jnp.zeros((FF,), jnp.float32),
    )
    d_state = cotangent.astype(jnp.float32) * valid[:, None].astype(jnp.float32)
    for turn in reversed(range(PASSES)):
        full = gather_weights(shards)

        def run_back(carry, full=full, kept=kept_all[turn]):
            d_in, added = backward_pass(carry[0], kept, full, visible)
            return (d_in, tuple((a + b for a, b in zip(carry[1], added))))

        def skip_back(carry):
            return carry

        d_state, grads = lax.cond(turn < passes_here, run_back, skip_back, (d_state, grads))
    groups_n = lax.axis_size("grp")
    rows_n = lax.axis_size("row")
    bias_order = grads[5].reshape(groups_n, rows_n, -1).transpose(1, 0, 2).reshape(-1)
    partial_sums = reduce_row((grads[0], grads[1], grads[2], grads[3], grads[4], bias_order))
    summed = reduce_grp(partial_sums)
    weighted = tuple((s / total for s in summed))
    keep_feat = 1.0 - reset_flag.astype(jnp.float32)
    row_count = w_qkv.shape[0]
    row_start = lax.axis_index("row") * row_count
    keep_rows = lax.dynamic_slice_in_dim(keep_feat, row_start, row_count)[:, None]
    col_count = vectors.shape[1]
    col_start = lax.axis_index("grp") * col_count
    keep_cols = lax.dynamic_slice_in_dim(keep_feat, col_start, col_count)[None, :]
    bias_count = fc_bias.shape[0]
    bias_start = (lax.axis_index("grp") * lax.axis_size("row") + lax.axis_index("row")) * bias_count
    bias_index = (bias_start + jnp.arange(bias_count, dtype=jnp.int32)) % D
    keep_bias = keep_feat[bias_index]
    keeps = (keep_rows, keep_rows, keep_rows, keep_cols, keep_cols, keep_bias)
    t_step = float(STEP)
    firsts = (first_qkv, first_out, first_fc, first_proj, first_vectors, first_fc_bias)
    seconds = (second_qkv, second_out, second_fc, second_proj, second_vectors, second_fc_bias)
    updated = [
        adam_update(w, m, v, g, kp, t_step)
        for w, m, v, g, kp in zip(shards, firsts, seconds, weighted, keeps)
    ]
    return (
        hidden,
        d_state,
        weighted[0],
        weighted[1],
        weighted[2],
        weighted[3],
        weighted[4],
        weighted[5],
        updated[0][0],
        updated[1][0],
        updated[2][0],
        updated[3][0],
        updated[4][0],
        updated[5][0],
        updated[0][1],
        updated[1][1],
        updated[2][1],
        updated[3][1],
        updated[4][1],
        updated[5][1],
        updated[0][2],
        updated[1][2],
        updated[2][2],
        updated[3][2],
        updated[4][2],
        updated[5][2],
    )


def solution(mesh):
    placed = (
        P(("grp", "row"), None),
        P(("grp", "row"), None),
        P("row", "grp"),
        P("row", "grp"),
        P("row", "grp"),
        P("row", "grp"),
        P("row", "grp"),
        P(("grp", "row")),
        P("row", "grp"),
        P("row", "grp"),
        P("row", "grp"),
        P("row", "grp"),
        P("row", "grp"),
        P(("grp", "row")),
        P("row", "grp"),
        P("row", "grp"),
        P("row", "grp"),
        P("row", "grp"),
        P("row", "grp"),
        P(("grp", "row")),
        P(("grp", "row"), None),
        P("grp"),
        P(),
    )
    return jax.shard_map(
        body,
        mesh=mesh,
        in_specs=placed,
        out_specs=(
            P(("grp", "row"), None),
            P(("grp", "row"), None),
            P("row", "grp"),
            P("row", "grp"),
            P("row", "grp"),
            P("row", "grp"),
            P("row", "grp"),
            P(("grp", "row")),
            P("row", "grp"),
            P("row", "grp"),
            P("row", "grp"),
            P("row", "grp"),
            P("row", "grp"),
            P(("grp", "row")),
            P("row", "grp"),
            P("row", "grp"),
            P("row", "grp"),
            P("row", "grp"),
            P("row", "grp"),
            P(("grp", "row")),
            P("row", "grp"),
            P("row", "grp"),
            P("row", "grp"),
            P("row", "grp"),
            P("row", "grp"),
            P(("grp", "row")),
        ),
        check_vma=False,
    )
```

profile of v0, /device:TPU:0, one launch (start us, length us, event | category | flops | bytes accessed | tf_op | source)
XLA Modules:
  0.0 1252.2 jit_solution(11232057236415350201)
XLA Ops:
  15.4 8.0 all_gather.26
  24.4 9.7 all_gather.30
  34.2 8.1 all_gather.34
  48.2 26.4 %all-gather.1 = bf16[8,96,8]{1,2,0:T(8,128)(2,1)S(1)} all-gather(bf16[1,96,8]{1,2,0:T(8,128)(2,1)S(1)} %bitcast.162), channel_id=1, replica_groups=mesh['grp'=8,'row'=4] {'grp'}, dimensions={0}, use_global_device_ids=true | all-gather | bytes 13824 | tf_op jit(solution)/shard_map/all_gather | solution.py:43
  82.4 26.5 %all-gather.2 = bf16[8,1,384]{2,1,0:T(2,128)(2,1)S(1)} all-gather(bf16[1,1,384]{2,1,0:T(2,128)(2,1)S(1)} %reshape.423), channel_id=1, replica_groups=mesh['grp'=8,'row'=4] {'grp'}, dimensions={0}, use_global_device_ids=true | all-gather | bytes 6912 | tf_op jit(solution)/shard_map/all_gather | solution.py:44
  111.9 13.0 %all-gather.8.cloned.1.call-done = bf16[768,2304]{0,1:T(8,128)(2,1)} async-done(((bf16[768,288]{0,1:T(8,128)(2,1)}), bf16[768,2304]{0,1:T(8,128)(2,1)}) %all-gather.8.cloned.1.call-update) | async-done | bytes 3538960 | tf_op jit(solution)/shard_map/all_gather | solution.py:39
  124.9 81.6 %all-gather.12.cloned.1.call-done = bf16[768,3072]{1,0:T(8,128)(2,1)} async-done(((bf16[768,384]{1,0:T(8,128)(2,1)}), bf16[768,3072]{1,0:T(8,128)(2,1)}) %all-gather.12.cloned.1.call-update) | async-done | bytes 4718608 | tf_op jit(solution)/shard_map/all_gather | solution.py:41
  206.5 80.1 %all-gather.14.cloned.1.call-done = bf16[3072,768]{0,1:T(8,128)(2,1)} async-done(((bf16[3072,96]{0,1:T(8,128)(2,1)}), bf16[3072,768]{0,1:T(8,128)(2,1)}) %all-gather.14.cloned.1.call-update) | async-done | bytes 4718608 | tf_op jit(solution)/shard_map/all_gather | solution.py:42
  286.6 52.8 %conditional.4 = (f32[512,768]{1,0:T(8,128)S(1)}, f32[512,768]{1,0:T(8,128)}, bf16[512,768]{1,0:T(8,128)(2,1)}, bf16[512,12,64]{0,2,1:T(8,128)(2,1)}, bf16[512,1...) conditional(s32[]{:T(128)} %bitcast.35, ...), branch_computations={%region_1.0_spmd, %region_2.9_spmd} | conditional | flops 8117161984 | bytes 171817248 | solution.py:232
  340.0 18.4 %conditional.5 = (f32[512,768]{1,0:T(8,128)S(1)}, f32[512,768]{1,0:T(8,128)}, bf16[512,768]{1,0:T(8,128)(2,1)}, bf16[512,12,64]{0,2,1:T(8,128)(2,1)}, bf16[512,1...) conditional(s32[]{:T(128)} %bitcast.34, ...), branch_computations={%region_9.0_spmd, %region_10.17_spmd} | conditional | flops 8117161984 | bytes 171817248 | solution.py:232
  359.6 16.4 %conditional.6 = (f32[512,768]{1,0:T(8,128)S(1)}, f32[768,2304]{0,1:T(8,128)}, f32[768,768]{0,1:T(8,128)}, f32[768,3072]{0,1:T(8,128)}, f32[3072,768]{1,0:T(8,12...) conditional(s32[]{:T(128)} %bitcast.34, f32[512,768]{1,0:T(8,128)S(1)} %convert_multiply_fusion, ...), branch_computations={%region_17.0_spmd, %region_18.37_spmd} | conditional | flops 16659006464 | bytes 334586304 | solution.py:254
  376.1 123.7 %conditional.7 = ((f32[512,768]{1,0:T(8,128)S(1)}, f32[768,2304]{0,1:T(8,128)}, f32[768,768]{0,1:T(8,128)}, f32[768,3072]{0,1:T(8,128)}, f32[3072,768]{1,0:T(8,1...) conditional(s32[]{:T(128)} %bitcast.35, (f32[512,768]{1,0:T(8,128)S(1)}, f32[768,2304]{0,1:T(8,128)}, ...), branch_computations={%region_37.0_spmd, %region_38.57_spmd} | conditional | flops 16666093568 | bytes 363008448 | solution.py:254
  376.1 10.9 convolution_add_fusion.2
  392.7 9.6 fusion.194
  420.5 7.8 fusion.201
  428.3 20.2 %fusion.138 = bf16[12,512,64]{1,2,0:T(8,128)(2,1)S(1)} fusion(bf16[512,12,64]{0,2,1:T(8,128)(2,1)} %get-tuple-element.174, f32[12,512,512]{1,2,0:T(8,128)} %fusion.201, f32[12,512,512]{1,2,0:T(8,128)} %copy-done.4, f32[12,512]{1,0:T(8,128)S(1)} %bitcast.157, pred[512,512]{0,1:T(8,128)(4,1)S(1)} %get-tuple-element.173), kind=kOutput, calls=%fused_computation.214 | convolution fusion | flops 437656064 | bytes 27025408 | tf_op jit(solution)/shard_map/cond/branch_1_fun/hqk,qhd->khd/dot_general | solution.py:150
  448.5 21.2 %bitcast_convert_fusion.3 = (bf16[512,12,64]{0,2,1:T(8,128)(2,1)}, f32[12,512,64]{1,2,0:T(8,128)}) fusion(bf16[512,12,64]{0,2,1:T(8,128)(2,1)} %get-tuple-element.175, f32[12,512,512]{1,2,0:T(8,128)} %fusion.201, f32[12,512,512]{1,2,0:T(8,128)} %copy-done.4, f32[12,512]{1,0:T(8,128)S(1)} %bitcast.158, pred[512,512]{0,1:T(8,128)(4,1)S(1)} %get-tuple-element.173), kind=kOutput, calls=%fused_computation.201 | convolution fusion | flops 437656064 | bytes 28598272 | tf_op jit(solution)/shard_map/cond/branch_1_fun/hqk,khd->qhd/dot_general | solution.py:147
  478.5 8.3 bitcast_add_fusion.1
  503.6 8.1 copy.249
  511.7 9.7 copy.251
  521.4 9.6 copy.252
  531.9 11.1 all-reduce.4
  544.0 124.6 %reduce-scatter.18.cloned.1.call-done = f32[192,768]{1,0:T(8,128)} async-done(((f32[768,768]{1,0:T(8,128)}), f32[192,768]{1,0:T(8,128)}) %reduce-scatter.18.cloned.1.call-update) | async-done | bytes 589840 | tf_op jit(solution)/shard_map/reduce_scatter | solution.py:62
  670.9 63.9 %reduce-scatter.16.cloned.1.call-done = f32[192,2304]{1,0:T(8,128)} async-done(((f32[768,2304]{1,0:T(8,128)}), f32[192,2304]{1,0:T(8,128)}) %reduce-scatter.16.cloned.1.call-update) | async-done | bytes 1769488 | tf_op jit(solution)/shard_map/reduce_scatter | solution.py:61
  737.8 78.1 %reduce-scatter.20.cloned.1.call-done = f32[192,3072]{1,0:T(8,128)} async-done(((f32[768,3072]{1,0:T(8,128)}), f32[192,3072]{1,0:T(8,128)}) %reduce-scatter.20.cloned.1.call-update) | async-done | bytes 2359312 | tf_op jit(solution)/shard_map/reduce_scatter | solution.py:63
  816.0 81.0 %reduce-scatter.24.cloned.1.call-done = f32[768,768]{0,1:T(8,128)} async-done(((f32[3072,768]{0,1:T(8,128)}), f32[768,768]{0,1:T(8,128)}) %reduce-scatter.24.cloned.1.call-update) | async-done | bytes 2359312 | tf_op jit(solution)/shard_map/reduce_scatter | solution.py:64
  898.3 39.7 %psum.7 = f32[]{:T(128)} all-reduce(f32[]{:T(128)} %fusion.172), channel_id=1, replica_groups=mesh['grp'=8,'row'=4] {'grp','row'}, use_global_device_ids=true, to_apply=%region_60.0 | all-reduce | flops 1 | bytes 8 | tf_op jit(solution)/shard_map/psum | solution.py:218
  943.4 21.3 %all-reduce.3 = f32[768]{0:T(1024)S(1)} all-reduce(f32[768]{0:T(1024)S(1)} %dynamic-slice.4), channel_id=13, replica_groups=mesh['grp'=8,'row'=4] {'grp'}, use_global_device_ids=true, to_apply=%region_70.0.clone | all-reduce | flops 768 | bytes 6144
  969.6 56.7 %reduce-scatter.30.cloned.1.call-done = f32[96,192]{1,0:T(8,128)} async-done(((f32[768,192]{1,0:T(8,128)}), f32[96,192]{1,0:T(8,128)}) %reduce-scatter.30.cloned.1.call-update) | async-done | bytes 73744
  1029.7 68.5 %reduce-scatter.28.cloned.1.call-done = f32[288,192]{1,0:T(8,128)} async-done(((f32[2304,192]{1,0:T(8,128)}), f32[288,192]{1,0:T(8,128)}) %reduce-scatter.28.cloned.1.call-update) | async-done | bytes 221200
  1101.3 69.1 %reduce-scatter.22.cloned.1.call-done = f32[192,384]{1,0:T(8,128)} async-done(((f32[192,3072]{1,0:T(8,128)}), f32[192,384]{1,0:T(8,128)}) %reduce-scatter.22.cloned.1.call-update) | async-done | bytes 294928 | tf_op jit(solution)/shard_map/reduce_scatter | solution.py:52
  1173.3 69.2 %reduce-scatter.26.cloned.1.call-done = f32[768,96]{0,1:T(8,128)} async-done(((f32[768,768]{0,1:T(8,128)}), f32[768,96]{0,1:T(8,128)}) %reduce-scatter.26.cloned.1.call-update) | async-done | bytes 294928 | tf_op jit(solution)/shard_map/reduce_scatter | solution.py:53
  (244 shorter events, 183.1 us)
Async XLA Ops:
  7.2 35.9 %copy-start.18 = (bf16[512,768]{1,0:T(8,128)(2,1)S(1)}, bf16[512,768]{1,0:T(8,128)(2,1)}, u32[]{:S(2)}) copy-start(bf16[512,768]{1,0:T(8,128)(2,1)} %param.31) | copy-start | bytes 2359300
  7.2 104.6 %all-gather.10.cloned.1.call-start = ((), (), s32[]{:S(2)}) async-start(), calls=%async_computation.10 | async-start | bytes 1327104 | tf_op jit(solution)/shard_map/all_gather | solution.py:40
  15.3 27.9 %copy-start.33 = (bf16[2,96]{1,0:T(2,128)(2,1)S(1)}, bf16[2,96]{1,0:T(2,128)(2,1)}, u32[]{:S(2)}) copy-start(bf16[2,96]{1,0:T(2,128)(2,1)} %param.37) | copy-start | bytes 1156
  15.3 59.5 %copy-start.34 = (u32[32]{0:T(128)S(1)}, u32[32]{0:T(128)}, u32[]{:S(2)}) copy-start(u32[32]{0:T(128)} %constant.261) | copy-start | bytes 388
  15.3 60.7 %copy-start.36 = (bf16[96]{0:T(256)(128)(2,1)S(1)}, bf16[96]{0:T(256)(128)(2,1)}, u32[]{:S(2)}) copy-start(bf16[96]{0:T(256)(128)(2,1)} %param.38) | copy-start | bytes 580
  15.3 93.6 %copy-start.35 = (s32[1,8]{1,0:T(1,128)S(1)}, s32[1,8]{1,0:T(1,128)}, u32[]{:S(2)}) copy-start(s32[1,8]{1,0:T(1,128)} %param.51) | copy-start | bytes 100
  15.3 109.6 %all-gather.8.cloned.1.call-start = ((), (), s32[]{:S(2)}) async-start(), calls=%async_computation.9 | async-start | bytes 3981312 | tf_op jit(solution)/shard_map/all_gather | solution.py:39
  24.4 182.1 %all-gather.12.cloned.1.call-start = ((), (), s32[]{:S(2)}) async-start(), calls=%async_computation.11 | async-start | bytes 5308416 | tf_op jit(solution)/shard_map/all_gather | solution.py:41
  34.2 252.5 %all-gather.14.cloned.1.call-start = ((), (), s32[]{:S(2)}) async-start(), calls=%async_computation.12 | async-start | bytes 5308416 | tf_op jit(solution)/shard_map/all_gather | solution.py:42
  42.4 626.3 %reduce-scatter.18.cloned.1.call-start = ((), (), s32[]{:S(2)}) async-start(), calls=%async_computation.14 | async-start | bytes 2949120 | tf_op jit(solution)/shard_map/reduce_scatter | solution.py:62
  420.5 49.3 %copy-start.13 = (bf16[512,12,64]{0,2,1:T(8,128)(2,1)}, bf16[512,12,64]{0,2,1:T(8,128)(2,1)S(1)}, u32[]{:S(2)}) copy-start(bf16[512,12,64]{0,2,1:T(8,128)(2,1)S(1)} %get-tuple-element.836) | copy-start | bytes 2359300 | tf_op jit(solution)/shard_map/cond
  503.5 231.3 %reduce-scatter.16.cloned.1.call-start = ((), (), s32[]{:S(2)}) async-start(), calls=%async_computation.13 | async-start | bytes 8847360 | tf_op jit(solution)/shard_map/reduce_scatter | solution.py:61
  511.6 304.2 %reduce-scatter.20.cloned.1.call-start = ((), (), s32[]{:S(2)}) async-start(), calls=%async_computation.15 | async-start | bytes 11796480 | tf_op jit(solution)/shard_map/reduce_scatter | solution.py:63
  521.4 375.6 %reduce-scatter.24.cloned.1.call-start = ((), (), s32[]{:S(2)}) async-start(), calls=%async_computation.17 | async-start | bytes 11796480 | tf_op jit(solution)/shard_map/reduce_scatter | solution.py:64
  531.1 435.7 %reduce-scatter.32.cloned.1.call-start = ((), (), s32[]{:S(2)}) async-start(), calls=%async_computation.21 | async-start | bytes 442368
  544.0 482.3 %reduce-scatter.30.cloned.1.call-start = ((), (), s32[]{:S(2)}) async-start(), calls=%async_computation.20 | async-start | bytes 884736
  670.9 427.4 %reduce-scatter.28.cloned.1.call-start = ((), (), s32[]{:S(2)}) async-start(), calls=%async_computation.19 | async-start | bytes 2654208
  737.7 200.9 %copy-start.48 = (u32[32]{0:T(128)S(1)}, u32[32]{0:T(128)}, u32[]{:S(2)}) copy-start(u32[32]{0:T(128)} %constant.275) | copy-start | bytes 388
  737.8 201.6 %copy-start.32 = (s32[768]{0:T(1024)S(1)}, s32[768]{0:T(1024)}, u32[]{:S(2)}) copy-start(s32[768]{0:T(1024)} %param.53) | copy-start | bytes 9220
  737.8 203.9 %copy-start.1 = (f32[512,768]{1,0:T(8,128)S(1)}, f32[512,768]{1,0:T(8,128)}, u32[]{:S(2)}) copy-start(f32[512,768]{1,0:T(8,128)} %copy-done) | copy-start | bytes 4718596
  737.8 432.7 %reduce-scatter.22.cloned.1.call-start = ((), (), s32[]{:S(2)}) async-start(), calls=%async_computation.16 | async-start | bytes 2654208 | tf_op jit(solution)/shard_map/reduce_scatter | solution.py:52
  815.9 211.4 %copy-start.29 = (bf16[192,96]{1,0:T(8,128)(2,1)S(1)}, bf16[192,96]{1,0:T(8,128)(2,1)}, u32[]{:S(2)}) copy-start(bf16[192,96]{1,0:T(8,128)(2,1)} %param.34) | copy-start | bytes 110596
  815.9 283.5 %copy-start.21 = (bf16[192,288]{1,0:T(8,128)(2,1)S(1)}, bf16[192,288]{1,0:T(8,128)(2,1)}, u32[]{:S(2)}) copy-start(bf16[192,288]{1,0:T(8,128)(2,1)} %param.33) | copy-start | bytes 331780
  815.9 283.5 %copy-start.23 = (f32[192,288]{1,0:T(8,128)S(1)}, f32[192,288]{1,0:T(8,128)}, u32[]{:S(2)}) copy-start(f32[192,288]{1,0:T(8,128)} %param.39) | copy-start | bytes 663556
  815.9 283.5 %copy-start.24 = (f32[192,288]{1,0:T(8,128)S(1)}, f32[192,288]{1,0:T(8,128)}, u32[]{:S(2)}) copy-start(f32[192,288]{1,0:T(8,128)} %param.45) | copy-start | bytes 663556
  816.0 426.6 %reduce-scatter.26.cloned.1.call-start = ((), (), s32[]{:S(2)}) async-start(), calls=%async_computation.18 | async-start | bytes 2654208 | tf_op jit(solution)/shard_map/reduce_scatter | solution.py:53
  897.0 273.4 %copy-start.22 = (bf16[192,384]{1,0:T(8,128)(2,1)S(1)}, bf16[192,384]{1,0:T(8,128)(2,1)}, u32[]{:S(2)}) copy-start(bf16[192,384]{1,0:T(8,128)(2,1)} %param.35) | copy-start | bytes 442372
  897.0 273.4 %copy-start.25 = (f32[192,384]{1,0:T(8,128)S(1)}, f32[192,384]{1,0:T(8,128)}, u32[]{:S(2)}) copy-start(f32[192,384]{1,0:T(8,128)} %param.41) | copy-start | bytes 884740
  897.0 273.4 %copy-start.26 = (f32[192,384]{1,0:T(8,128)S(1)}, f32[192,384]{1,0:T(8,128)}, u32[]{:S(2)}) copy-start(f32[192,384]{1,0:T(8,128)} %param.47) | copy-start | bytes 884740
  941.6 301.0 %copy-start.20 = (bf16[768,96]{0,1:T(8,128)(2,1)S(1)}, bf16[768,96]{0,1:T(8,128)(2,1)}, u32[]{:S(2)}) copy-start(bf16[768,96]{0,1:T(8,128)(2,1)} %param.36) | copy-start | bytes 442372
  941.6 301.0 %copy-start.27 = (f32[768,96]{0,1:T(8,128)S(1)}, f32[768,96]{0,1:T(8,128)}, u32[]{:S(2)}) copy-start(f32[768,96]{0,1:T(8,128)} %param.42) | copy-start | bytes 884740
  942.6 300.0 %copy-start.28 = (f32[768,96]{0,1:T(8,128)S(1)}, f32[768,96]{0,1:T(8,128)}, u32[]{:S(2)}) copy-start(f32[768,96]{0,1:T(8,128)} %param.48) | copy-start | bytes 884740
  (24 other events, 173.3 us)
Sparse Core Ops, SparseCore 0:
  15.4 42.5 all-gather.9
  60.8 64.0 all-gather.7
  127.0 79.4 all-gather.11
  208.5 78.0 all-gather.13
  503.6 164.9 reduce-scatter.17
  671.2 63.6 reduce-scatter.15
  737.4 78.4 reduce-scatter.19
  818.5 78.4 reduce-scatter.23
  900.2 61.3 reduce-scatter.31
  964.8 61.4 reduce-scatter.29
  1030.2 68.0 reduce-scatter.27
  1102.0 68.3 reduce-scatter.21
  1174.3 68.1 reduce-scatter.25
where the time goes:
time: 1260 us; the launch traced here: 1250 us
  waiting for transfers between devices  786 us (62%)
  blocking collectives  169 us (13%)
  matrix products  138 us (11%)
  local copies, waits for them, and re-layouts  91.8 us (7%)
  other arithmetic  39.8 us (3%)
  between operations  17.8 us (1%)
    unnamed x16, waiting for transfers between devices  125 us
    reduce_scatter x1, waiting for transfers between devices, reduce_row(): lax.psum_scatter(parts[1], 'row', scatter_dimension=0, tiled=True)  125 us
    all_gather x1, waiting for transfers between devices, gather_weights(): lax.all_gather(rows[2], 'grp', axis=1, tiled=True)  81.6 us
    reduce_scatter x1, waiting for transfers between devices, reduce_row(): lax.psum_scatter(parts[3], 'row', scatter_dimension=0, tiled=True)  81 us
    all_gather x1, waiting for transfers between devices, gather_weights(): lax.all_gather(rows[3], 'grp', axis=1, tiled=True)  80.1 us
    reduce_scatter x1, waiting for transfers between devices, reduce_row(): lax.psum_scatter(parts[2], 'row', scatter_dimension=0, tiled=True)  78.1 us
    reduce_scatter x1, waiting for transfers between devices, reduce_grp(): lax.psum_scatter(parts[3], 'grp', scatter_dimension=1, tiled=True)  69.2 us
    reduce_scatter x1, waiting for transfers between devices, reduce_grp(): lax.psum_scatter(parts[2], 'grp', scatter_dimension=1, tiled=True)  69.1 us
  transfers between devices with their start and end apart: 13, of which 11 were waited for; matrix products, arithmetic and copies ran while one was open for 5% of the time, Pallas kernels for 0%

commit v1 on v0

v1 whole, which is shorter than its diff:
```python
import functools

import jax
import jax.numpy as jnp
from jax import lax
from jax.experimental import pallas as pl
from jax.experimental.pallas import tpu as pltpu
from jax.sharding import PartitionSpec as P

D = 768
HEADS = 12
HEAD = 64
FF = 3072
STEP = 10
LEARN_RATE = 0.03
WEIGHT_DECAY = 0.1
F32 = jnp.float32
BF16 = jnp.bfloat16
NN = (((1,), (0,)), ((), ()))
NT = (((1,), (1,)), ((), ()))
TN = (((0,), (0,)), ((), ()))
NB = 256
EXTRA = 16
GELU_A = 0.7978845608028654
GELU_B = 0.044715
BOTH = ("grp", "row")

VM = pl.BlockSpec(memory_space=pltpu.VMEM)
SM = pl.BlockSpec(memory_space=pltpu.SMEM)
HB = pl.BlockSpec(memory_space=pl.ANY)
PARAMS = pltpu.CompilerParams(vmem_limit_bytes=60 * 2**20)


def like(shape, dtype):
    return jax.ShapeDtypeStruct(shape, dtype)


def mm(a, b, dims):
    return lax.dot_general(a, b, dims, preferred_element_type=F32)


def kernel_call(body, outs, specs, scratch=(), out_specs=None):
    return pl.pallas_call(
        body,
        out_shape=outs,
        in_specs=specs,
        out_specs=out_specs or [VM] * len(outs),
        scratch_shapes=list(scratch),
        compiler_params=PARAMS,
    )


def norm_stats(x):
    centred = x - jnp.mean(x, -1, keepdims=True)
    inv = lax.rsqrt(jnp.mean(centred * centred, -1, keepdims=True) + 1e-5)
    return centred * inv, inv


def colsum(x):
    return jnp.sum(x, 0, keepdims=True)


def fill_mask(ends_ref, mask_ref):
    tokens = mask_ref.shape[0]
    n_ends = ends_ref.shape[1]

    def segments(pos):
        seg = jnp.zeros(pos.shape, jnp.int32)
        for e in range(n_ends):
            seg += (pos >= ends_ref[0, e]).astype(jnp.int32)
        return seg

    seg_keys = segments(lax.broadcasted_iota(jnp.int32, (1, tokens), 1))
    for i in range(0, tokens, 128):
        pos = lax.broadcasted_iota(jnp.int32, (128, 1), 0) + i
        key = lax.broadcasted_iota(jnp.int32, (128, tokens), 1)
        seen = (segments(pos) == seg_keys) & (key <= pos)
        mask_ref[i : i + 128, :] = jnp.where(seen, 0.0, -1e30)


def attention_forward(h, wqkv, wout, vec, mask, a, qkv, lse, mixed, h_mid, tile=256):
    tokens = h.shape[0]
    xhat, _ = norm_stats(h[...].astype(F32))
    a[...] = (xhat * vec[0:1, :] + vec[1:2, :]).astype(BF16)
    for part in range(3):
        for j in range(0, D, NB):
            o = part * D + j
            r = mm(a[...], wqkv[:, o : o + NB], NN)
            if part == 0:
                r = r + vec[2:3, j : j + NB]
            if part == 2:
                r = r + vec[3:4, j : j + NB]
            qkv[:, o : o + NB] = r.astype(BF16)
    lanes = lax.broadcasted_iota(jnp.int32, (tile, 128), 1)
    low = lanes < HEAD
    for i in range(tokens // tile):
        rows = slice(i * tile, (i + 1) * tile)
        seen = (i + 1) * tile
        lse[rows, :] = jnp.zeros((tile, 128), F32)
        for p in range(HEADS // 2):
            c = 128 * p
            q = qkv[rows, c : c + 128] * BF16(HEAD**-0.5)
            k = qkv[0:seen, D + c : D + c + 128]
            v = qkv[0:seen, 2 * D + c : 2 * D + c + 128]
            outs = []
            for half in range(2):
                own = low if half == 0 else ~low
                s = mm(jnp.where(own, q, BF16(0)), k, NT) + mask[rows, 0:seen]
                top = jnp.max(s, -1, keepdims=True)
                e = jnp.exp(s - top)
                den = jnp.sum(e, -1, keepdims=True)
                outs.append(mm(e.astype(BF16), v, NN) / den)
                lse[rows, :] = jnp.where(lanes == 2 * p + half, top + jnp.log(den), lse[rows, :])
            mixed[rows, c : c + 128] = jnp.where(low, outs[0], outs[1]).astype(BF16)
    for j in range(0, D, NB):
        r = mm(mixed[...], wout[:, j : j + NB], NN)
        h_mid[:, j : j + NB] = h[:, j : j + NB].astype(F32) + r + vec[4:5, j : j + NB]


def ffn_forward(h_mid, wfc, wpt, vec, fb, c, g, gp, h_out):
    xhat, _ = norm_stats(h_mid[...])
    c[...] = (xhat * vec[5:6, :] + vec[6:7, :]).astype(BF16)
    for j in range(0, FF, NB):
        f = mm(c[...], wfc[:, j : j + NB], NN) + fb[0:1, j : j + NB]
        sq = f * f
        t = jnp.tanh(GELU_A * (f + GELU_B * sq * f))
        half = 0.5 * (1.0 + t)
        g[:, j : j + NB] = (f * half).astype(BF16)
        slope = half + (0.5 * GELU_A) * f * (1.0 - t * t) * (1.0 + (3 * GELU_B) * sq)
        gp[:, j : j + NB] = slope.astype(BF16)
    for j in range(0, D, NB):
        r = mm(g[...], wpt[j : j + NB, :], NT)
        h_out[:, j : j + NB] = h_mid[:, j : j + NB] + r + vec[7:8, j : j + NB]


def norm_backward(dout, x, gain):
    xhat, inv = norm_stats(x)
    d_gain = colsum(dout * xhat)
    d_bias = colsum(dout)
    dx = dout * gain
    m1 = jnp.mean(dx, -1, keepdims=True)
    m2 = jnp.mean(dx * xhat, -1, keepdims=True)
    return inv * (dx - m1 - xhat * m2), d_gain, d_bias


def ffn_backward(dy, h_mid, gp, wfc, wpt, vec, dy_low, df_low, dfb, dh_mid, dh_low, dvec, dc):
    d_out = dy[...]
    dy_low[...] = d_out.astype(BF16)
    dvec[0:4, :] = jnp.zeros((4, D), F32)
    dvec[7:8, :] = colsum(d_out)
    for j in range(0, FF, NB):
        d = mm(dy_low[...], wpt[:, j : j + NB], NN)
        df = d * gp[:, j : j + NB].astype(F32)
        dfb[0:1, j : j + NB] = colsum(df)
        df_low[:, j : j + NB] = df.astype(BF16)
    for j in range(0, D, NB):
        dc[:, j : j + NB] = mm(df_low[...], wfc[j : j + NB, :], NT)
    dx, d_gain, d_bias = norm_backward(dc[...], h_mid[...], vec[5:6, :])
    total = dy[...] + dx
    dh_mid[...] = total
    dh_low[...] = total.astype(BF16)
    dvec[4:5, :] = colsum(total)
    dvec[5:6, :] = d_gain
    dvec[6:7, :] = d_bias


def attention_backward(
    dh_mid, dh_low, h, qkv, lse, mixed, mask, wqkv, wout, vec, dmix, dqkv, da, d_in, dvec
):
    tokens = h.shape[0]
    for j in range(0, D, NB):
        dmix[:, j : j + NB] = mm(dh_low[...], wout[j : j + NB, :], NT).astype(BF16)
    low = lax.broadcasted_iota(jnp.int32, (tokens, 128), 1) < HEAD
    low_rows = lax.broadcasted_iota(jnp.int32, (128, tokens), 0) < HEAD
    for p in range(HEADS // 2):
        c = 128 * p
        cs = slice(c, c + 128)
        q = qkv[:, cs] * BF16(HEAD**-0.5)
        k = qkv[:, D + c : D + c + 128]
        v = qkv[:, 2 * D + c : 2 * D + c + 128]
        dm = dmix[:, cs]
        prod = dm.astype(F32) * mixed[:, cs].astype(F32)
        dm_t = dm.astype(F32).T.astype(BF16)
        q_t = q.astype(F32).T.astype(BF16)
        dq = jnp.zeros((tokens, 128), F32)
        dk_t = jnp.zeros((128, tokens), F32)
        dv_t = jnp.zeros((128, tokens), F32)
        for half in range(2):
            own = low if half == 0 else ~low
            own_rows = low_rows if half == 0 else ~low_rows
            delta = jnp.sum(jnp.where(own, prod, 0.0), -1, keepdims=True)
            s = mm(jnp.where(own, q, BF16(0)), k, NT) + mask[...]
            probs = jnp.exp(s - lse[:, 2 * p + half : 2 * p + half + 1])
            dp = mm(jnp.where(own, dm, BF16(0)), v, NT)
            ds = (probs * (dp - delta)).astype(BF16)
            dv_t += mm(jnp.where(own_rows, dm_t, BF16(0)), probs.astype(BF16), NN)
            dk_t += mm(jnp.where(own_rows, q_t, BF16(0)), ds, NN)
            dq += mm(ds, jnp.where(own, k, BF16(0)), NN)
        dq = dq * HEAD**-0.5
        dv = dv_t.T
        dvec[2:3, cs] = colsum(dq)
        dvec[3:4, cs] = colsum(dv)
        dqkv[:, cs] = dq.astype(BF16)
        dqkv[:, D + c : D + c + 128] = dk_t.T.astype(BF16)
        dqkv[:, 2 * D + c : 2 * D + c + 128] = dv.astype(BF16)
    for j in range(0, D, NB):
        da[:, j : j + NB] = mm(dqkv[...], wqkv[j : j + NB, :], NT)
    dx, d_gain, d_bias = norm_backward(da[...], h[...].astype(F32), vec[0:1, :])
    d_in[...] = dh_mid[...] + dx
    dvec[4:8, :] = jnp.zeros((4, D), F32)
    dvec[0:1, :] = d_gain
    dvec[1:2, :] = d_bias


def attention_forward_call(ends, h, wqkv, wout, vec):
    t = h.shape[0]

    def body(ends, h, wqkv, wout, vec, a, qkv, lse, mixed, h_mid, mask):
        fill_mask(ends, mask)
        attention_forward(h, wqkv, wout, vec, mask, a, qkv, lse, mixed, h_mid)

    outs = [
        like((t, D), BF16),
        like((t, 3 * D), BF16),
        like((t, 128), F32),
        like((t, D), BF16),
        like((t, D), F32),
    ]
    return kernel_call(body, outs, [SM, VM, VM, VM, VM], [pltpu.VMEM((t, t), F32)])(
        ends, h, wqkv, wout, vec
    )


def ffn_forward_call(h_mid, wfc, wpt, vec, fb):
    t = h_mid.shape[0]
    outs = [like((t, D), BF16), like((t, FF), BF16), like((t, FF), BF16), like((t, D), F32)]
    return kernel_call(ffn_forward, outs, [VM] * 5)(h_mid, wfc, wpt, vec, fb)


def ffn_backward_call(dy, h_mid, gp, wfc, wpt, vec):
    t = dy.shape[0]
    outs = [
        like((t, D), BF16),
        like((t, FF), BF16),
        like((1, FF), F32),
        like((t, D), F32),
        like((t, D), BF16),
        like((8, D), F32),
    ]
    return kernel_call(ffn_backward, outs, [VM] * 6, [pltpu.VMEM((t, D), F32)])(
        dy, h_mid, gp, wfc, wpt, vec
    )


def attention_backward_call(ends, dh_mid, dh_low, h, qkv, lse, mixed, wqkv, wout, vec):
    t = h.shape[0]

    def body(
        ends, dh_mid, dh_low, h, qkv, lse, mixed, wqkv, wout, vec, dqkv, d_in, dvec, mask, dmix, da
    ):
        fill_mask(ends, mask)
        attention_backward(
            dh_mid, dh_low, h, qkv, lse, mixed, mask, wqkv, wout, vec, dmix, dqkv, da, d_in, dvec
        )

    outs = [like((t, 3 * D), BF16), like((t, D), F32), like((8, D), F32)]
    scratch = [pltpu.VMEM((t, t), F32), pltpu.VMEM((t, D), BF16), pltpu.VMEM((t, D), F32)]
    return kernel_call(body, outs, [SM] + [VM] * 9, scratch)(
        ends, dh_mid, dh_low, h, qkv, lse, mixed, wqkv, wout, vec
    )


class Cube:
    def __init__(self, groups, rows):
        self.groups, self.rows = groups, rows
        self.n = groups * rows
        self.bits = self.n.bit_length() - 1
        far = list(range(self.bits - 1, 2, -1))
        self.gather_plans = (far + [2, 1], far + [1, 2])
        self.scatter_plans = tuple(list(reversed(p)) for p in self.gather_plans)
        self.half = self.n // 2

    def swap(self, x, plans, step):
        pairs = [(i, i ^ (1 << plans[i & 1][step])) for i in range(self.n)]
        return lax.ppermute(x, BOTH, pairs)

    def swap_core(self, x):
        return lax.ppermute(x, BOTH, [(i, i ^ 1) for i in range(self.n)])

    def gather(self, block):
        held = block[None]
        for step in range(self.bits - 1):
            held = jnp.concatenate([held, self.swap(held, self.gather_plans, step)], 0)
        return held, self.swap_core(held)

    def scatter(self, slots):
        held = slots[: self.half] + self.swap_core(slots[self.half :])
        for step in range(self.bits - 1):
            mid = held.shape[0] // 2
            got = self.swap(held[mid:], self.scatter_plans, step)
            held = held[:mid] + got
        return held[0]

    def gather_source(self, me, side, slot):
        core = (me & 1) ^ side
        dest = me ^ side
        for k in range(self.bits - 1):
            if (slot >> k) & 1:
                flip0, flip1 = 1 << self.gather_plans[0][k], 1 << self.gather_plans[1][k]
                dest = dest ^ jnp.where(core == 1, flip1, flip0)
        return dest

    def scatter_slot(self, me, dest):
        rel = me ^ dest
        core = dest & 1
        slot = (rel & 1) * self.half
        for k in range(self.bits - 1):
            place = self.bits - 2 - k
            b0 = (rel >> self.scatter_plans[0][k]) & 1
            b1 = (rel >> self.scatter_plans[1][k]) & 1
            slot = slot + (jnp.where(core == 1, b1, b0) << place)
        return slot


def my_number(cube):
    return lax.axis_index("grp") * cube.rows + lax.axis_index("row")


def canonical(cube, held, other):
    me = my_number(cube)
    ids = [cube.gather_source(me, side, s) for side in (0, 1) for s in range(cube.half)]
    return jnp.zeros((cube.n,) + held.shape[1:], held.dtype).at[jnp.stack(ids)].set(
        jnp.concatenate([held, other], 0)
    )


def fits(rows, cols):
    return rows % 16 == 0 and cols % 128 == 0


def place_blocks(cube, held, other, sem, target):
    me = my_number(cube)
    copies = []
    for side, src in enumerate((held, other)):
        for s in range(cube.half):
            dev = cube.gather_source(me, side, s)
            copies.append(
                pltpu.make_async_copy(src.at[s], target(dev // cube.rows, dev % cube.rows), sem)
            )
    for cp in copies:
        cp.start()
    for cp in copies:
        cp.wait()


def assemble_fc(cube, held, other):
    br, bc = held.shape[1:]
    if not fits(br, bc):
        full = canonical(cube, held, other).reshape(cube.groups, cube.rows, br, bc)
        return full.transpose(1, 2, 0, 3).reshape(cube.rows * br, cube.groups * bc)

    def body(held, other, out, sem):
        def target(g, r):
            return out.at[pl.ds(pl.multiple_of(r * br, 16), br), pl.ds(pl.multiple_of(g * bc, 128), bc)]

        place_blocks(cube, held, other, sem, target)

    outs = [like((cube.rows * br, cube.groups * bc), BF16)]
    return kernel_call(body, outs, [HB, HB], [pltpu.SemaphoreType.DMA], [HB])(held, other)[0]


def assemble_proj(cube, held, other):
    br, bc = held.shape[1:]
    if not fits(br, bc):
        full = canonical(cube, held, other).reshape(cube.groups, cube.rows, br, bc)
        return full.transpose(0, 2, 1, 3).reshape(cube.groups * br, cube.rows * bc)

    def body(held, other, out, sem):
        def target(g, r):
            return out.at[pl.ds(pl.multiple_of(g * br, 16), br), pl.ds(pl.multiple_of(r * bc, 128), bc)]

        place_blocks(cube, held, other, sem, target)

    outs = [like((cube.groups * br, cube.rows * bc), BF16)]
    return kernel_call(body, outs, [HB, HB], [pltpu.SemaphoreType.DMA], [HB])(held, other)[0]


def assemble_attn(cube, held, other, sizes):
    bq, bo, rows_w, vrows, vcols, bias = sizes
    g_n, r_n = cube.groups, cube.rows
    br, bc = held.shape[1:]
    if not fits(br, bc):
        full = canonical(cube, held, other).reshape(g_n, r_n, br, bc)
        body_part = full[:, :, :rows_w]
        wqkv = body_part[..., :bq].transpose(1, 2, 0, 3).reshape(r_n * rows_w, g_n * bq)
        wout = body_part[..., bq : bq + bo].transpose(1, 2, 0, 3).reshape(r_n * rows_w, g_n * bo)
        ext = full[:, :, rows_w:].astype(F32)
        vec = ext[:, :, :vrows, :vcols].transpose(1, 2, 0, 3).reshape(r_n * vrows, g_n * vcols)
        fb = ext[:, :, vrows, :bias].reshape(1, g_n * r_n * bias)
        total = jnp.sum(ext[:, :, vrows + 1, 0]) * 16.0 + jnp.sum(ext[:, :, vrows + 1, 1])
        return wqkv, wout, vec, fb, jnp.full((8, 128), total, F32)

    def body(held, other, wqkv, wout, vec, fb, tot, blk, sem):
        def target(g, r):
            return blk.at[g, pl.ds(pl.multiple_of(r * br, 16), br)]

        place_blocks(cube, held, other, sem, target)
        count = jnp.zeros((1, 128), F32)
        for g in range(g_n):
            for r in range(r_n):
                rows = slice(r * rows_w, (r + 1) * rows_w)
                wqkv[rows, g * bq : (g + 1) * bq] = blk[g, r * br : r * br + rows_w, 0:bq]
                wout[rows, g * bo : (g + 1) * bo] = blk[g, r * br : r * br + rows_w, bq : bq + bo]
                ext = blk[g, r * br + rows_w : r * br + rows_w + EXTRA, :].astype(F32)
                vec[r * vrows : (r + 1) * vrows, g * vcols : (g + 1) * vcols] = ext[0:vrows, 0:vcols]
                at = (g * r_n + r) * bias
                fb[0:1, at : at + bias] = ext[vrows : vrows + 1, 0:bias]
                count += ext[vrows + 1 : vrows + 2, 0:128]
        lane = lax.broadcasted_iota(jnp.int32, (1, 128), 1)
        weight = jnp.where(lane == 0, 16.0, jnp.where(lane == 1, 1.0, 0.0))
        tot[...] = jnp.broadcast_to(jnp.sum(count * weight, -1, keepdims=True), (8, 128))

    outs = [
        like((r_n * rows_w, g_n * bq), BF16),
        like((r_n * rows_w, g_n * bo), BF16),
        like((r_n * vrows, g_n * vcols), F32),
        like((1, g_n * r_n * bias), F32),
        like((8, 128), F32),
    ]
    scratch = [pltpu.VMEM((g_n, r_n * br, bc), BF16), pltpu.SemaphoreType.DMA]
    return kernel_call(body, outs, [HB, HB], scratch)(held, other)


def ordered_slots(cube, blocks):
    me = my_number(cube)
    slots = jnp.stack([cube.scatter_slot(me, dest) for dest in range(cube.n)])
    return jnp.zeros_like(blocks).at[slots].set(blocks)


def stacked_t(parts, out):
    t = parts[0].shape[0]
    for i, part in enumerate(parts):
        out[:, i * t : (i + 1) * t] = part[...].astype(F32).T.astype(BF16)


def grad_fc_blocks(cube, c1, c0, df1, df0, br, bc):
    if not fits(br, bc):
        full = mm(c1, df1, TN) + mm(c0, df0, TN)
        full = full.astype(BF16).reshape(cube.rows, br, cube.groups, bc).transpose(2, 0, 1, 3)
        return ordered_slots(cube, full.reshape(cube.n, br, bc))
    t = c1.shape[0]

    def body(c1, c0, df1, df0, out, ct):
        me = my_number(cube)
        stacked_t((c1, c0), ct)
        for g in range(cube.groups):
            cols = slice(g * bc, (g + 1) * bc)
            full = mm(ct[:, 0:t], df1[:, cols], NN) + mm(ct[:, t : 2 * t], df0[:, cols], NN)
            full = full.astype(BF16)
            for r in range(cube.rows):
                slot = cube.scatter_slot(me, g * cube.rows + r)
                out[slot] = full[r * br : (r + 1) * br]

    outs = [like((cube.n, br, bc), BF16)]
    return kernel_call(body, outs, [VM] * 4, [pltpu.VMEM((D, 2 * t), BF16)])(c1, c0, df1, df0)[0]


def grad_proj_blocks(cube, dy1, dy0, g1, g0, br, bc):
    if not fits(br, bc):
        full = mm(dy1, g1, TN) + mm(dy0, g0, TN)
        full = full.astype(BF16).reshape(cube.groups, br, cube.rows, bc).transpose(0, 2, 1, 3)
        return ordered_slots(cube, full.reshape(cube.n, br, bc))
    t = dy1.shape[0]

    def body(dy1, dy0, g1, g0, out, dyt):
        me = my_number(cube)
        stacked_t((dy1, dy0), dyt)
        for r in range(cube.rows):
            cols = slice(r * bc, (r + 1) * bc)
            full = mm(dyt[:, 0:t], g1[:, cols], NN) + mm(dyt[:, t : 2 * t], g0[:, cols], NN)
            full = full.astype(BF16)
            for g in range(cube.groups):
                slot = cube.scatter_slot(me, g * cube.rows + r)
                out[slot] = full[g * br : (g + 1) * br]

    outs = [like((cube.n, br, bc), BF16)]
    return kernel_call(body, outs, [VM] * 4, [pltpu.VMEM((D, 2 * t), BF16)])(dy1, dy0, g1, g0)[0]


def grad_attn_blocks(cube, a1, a0, dq1, dq0, m1, m0, dh1, dh0, dvec, dfb, sizes, br, bc):
    bq, bo, rows_w, vrows, vcols, bias = sizes
    g_n, r_n = cube.groups, cube.rows
    if not fits(br, bc):
        dqkv = mm(a1, dq1, TN) + mm(a0, dq0, TN)
        dout = mm(m1, dh1, TN) + mm(m0, dh0, TN)
        wide = jnp.concatenate(
            [dqkv.reshape(r_n, rows_w, g_n, bq), dout.reshape(r_n, rows_w, g_n, bo)], -1
        ).transpose(2, 0, 1, 3)
        vecs = dvec.reshape(r_n, vrows, g_n, vcols).transpose(2, 0, 1, 3)
        biases = dfb.reshape(g_n, r_n, 1, bias)
        ext = jnp.zeros((g_n, r_n, EXTRA, bc), F32)
        ext = ext.at[:, :, :vrows, :vcols].set(vecs).at[:, :, vrows : vrows + 1, :bias].set(biases)
        full = jnp.concatenate([wide, ext], 2).astype(BF16)
        return ordered_slots(cube, full.reshape(cube.n, br, bc))
    t = a1.shape[0]

    def body(a1, a0, dq1, dq0, m1, m0, dh1, dh0, dvec, dfb, out, lt, wide):
        me = my_number(cube)
        stacked_t((a1, a0), lt)
        for j in range(0, 3 * D, NB):
            cols = slice(j, j + NB)
            full = mm(lt[:, 0:t], dq1[:, cols], NN) + mm(lt[:, t : 2 * t], dq0[:, cols], NN)
            wide[:, cols] = full.astype(BF16)
        stacked_t((m1, m0), lt)
        for j in range(0, D, NB):
            cols = slice(j, j + NB)
            full = mm(lt[:, 0:t], dh1[:, cols], NN) + mm(lt[:, t : 2 * t], dh0[:, cols], NN)
            wide[:, 3 * D + j : 3 * D + j + NB] = full.astype(BF16)
        for g in range(g_n):
            for r in range(r_n):
                slot = cube.scatter_slot(me, g * r_n + r)
                rows = slice(r * rows_w, (r + 1) * rows_w)
                out[slot, 0:rows_w, 0:bq] = wide[rows, g * bq : (g + 1) * bq]
                out[slot, 0:rows_w, bq : bq + bo] = wide[rows, 3 * D + g * bo : 3 * D + (g + 1) * bo]
                vecs = dvec[r * vrows : (r + 1) * vrows, g * vcols : (g + 1) * vcols]
                at = (g * r_n + r) * bias
                ext = jnp.concatenate(
                    [
                        jnp.concatenate([vecs, jnp.zeros((vrows, bc - vcols), F32)], 1),
                        jnp.concatenate([dfb[0:1, at : at + bias], jnp.zeros((1, bc - bias), F32)], 1),
                        jnp.zeros((EXTRA - vrows - 1, bc), F32),
                    ],
                    0,
                )
                out[slot, rows_w : rows_w + EXTRA, :] = ext.astype(BF16)

    outs = [like((cube.n, br, bc), BF16)]
    scratch = [pltpu.VMEM((D, 2 * t), BF16), pltpu.VMEM((D, 4 * D), BF16)]
    return kernel_call(body, outs, [VM] * 10, scratch)(a1, a0, dq1, dq0, m1, m0, dh1, dh0, dvec, dfb)[0]


def adam_update(weight, first, second, grad, keep_frac):
    t_step = float(STEP)
    first_new = 0.9 * first * keep_frac + 0.1 * grad
    second_new = 0.95 * second * keep_frac + 0.05 * grad * grad
    first_hat = first_new / (1.0 - 0.9**t_step)
    second_hat = second_new / (1.0 - 0.95**t_step)
    weight_new = weight.astype(F32) * (1.0 - LEARN_RATE * WEIGHT_DECAY) - LEARN_RATE * first_hat / (
        jnp.sqrt(second_hat) + 1e-08
    )
    return (weight_new.astype(BF16), first_new, second_new)


def body(
    hidden_in,
    cotangent,
    w_qkv,
    w_out,
    w_fc,
    w_proj,
    vectors,
    fc_bias,
    first_qkv,
    first_out,
    first_fc,
    first_proj,
    first_vectors,
    first_fc_bias,
    second_qkv,
    second_out,
    second_fc,
    second_proj,
    second_vectors,
    second_fc_bias,
    seg_ends,
    pass_counts,
    reset_flag,
):
    cube = Cube(lax.axis_size("grp"), lax.axis_size("row"))
    rows_w, bq = w_qkv.shape
    bo = w_out.shape[1]
    vrows, vcols = vectors.shape
    bias = fc_bias.shape[0]
    sizes = (bq, bo, rows_w, vrows, vcols, bias)
    wide = bq + bo
    length = hidden_in.shape[0]
    n_valid = seg_ends[0, -1]

    ext = jnp.zeros((EXTRA, wide), BF16)
    ext = lax.dynamic_update_slice(ext, vectors, (0, 0))
    ext = lax.dynamic_update_slice(ext, fc_bias[None], (vrows, 0))
    split = jnp.stack([n_valid // 16, n_valid % 16]).astype(BF16)[None]
    ext = lax.dynamic_update_slice(ext, split, (vrows + 1, 0))
    block_a = jnp.concatenate([jnp.concatenate([w_qkv, w_out], 1), ext], 0)
    wqkv, wout, vec, fb, tot = assemble_attn(cube, *cube.gather(block_a), sizes)
    wfc = assemble_fc(cube, *cube.gather(w_fc))
    wpt = assemble_proj(cube, *cube.gather(w_proj.T))
    total = tot[0, 0]

    active = pass_counts[0] > 1
    h0 = hidden_in
    a0, qkv0, lse0, mixed0, mid0 = attention_forward_call(seg_ends, h0, wqkv, wout, vec)
    c0, g0, gp0, h1 = ffn_forward_call(mid0, wfc, wpt, vec, fb)
    a1, qkv1, lse1, mixed1, mid1 = attention_forward_call(seg_ends, h1, wqkv, wout, vec)
    c1, g1, gp1, h2 = ffn_forward_call(mid1, wfc, wpt, vec, fb)
    hidden = jnp.where(active, h2, h1).astype(BF16)

    valid = (jnp.arange(length, dtype=jnp.int32) < n_valid)[:, None]
    d2 = jnp.where(valid, cotangent.astype(F32), 0.0)
    dy1 = jnp.where(active, d2, 0.0)
    dyl1, dfl1, dfb1, dhm1, dhl1, dvf1 = ffn_backward_call(dy1, mid1, gp1, wfc, wpt, vec)
    dqkv1, din1, dva1 = attention_backward_call(
        seg_ends, dhm1, dhl1, h1, qkv1, lse1, mixed1, wqkv, wout, vec
    )
    d1 = jnp.where(active, din1, d2)
    dyl0 = d1.astype(BF16)
    sum_p = cube.scatter(grad_proj_blocks(cube, dyl1, dyl0, g1, g0, vcols, w_proj.shape[0]))
    dyl0, dfl0, dfb0, dhm0, dhl0, dvf0 = ffn_backward_call(d1, mid0, gp0, wfc, wpt, vec)
    sum_f = cube.scatter(grad_fc_blocks(cube, c1, c0, dfl1, dfl0, *w_fc.shape))
    dqkv0, input_grad, dva0 = attention_backward_call(
        seg_ends, dhm0, dhl0, h0, qkv0, lse0, mixed0, wqkv, wout, vec
    )
    dvec = dvf1 + dva1 + dvf0 + dva0
    dfb = dfb1 + dfb0
    sum_a = cube.scatter(
        grad_attn_blocks(
            cube, a1, a0, dqkv1, dqkv0, mixed1, mixed0, dhl1, dhl0, dvec, dfb, sizes, rows_w + EXTRA, wide
        )
    )

    sum_a = sum_a.astype(F32)
    summed = (
        sum_a[:rows_w, :bq],
        sum_a[:rows_w, bq:],
        sum_f.astype(F32),
        sum_p.T.astype(F32),
        sum_a[rows_w : rows_w + vrows, :vcols],
        sum_a[rows_w + vrows, :bias],
    )
    grads = tuple(s / total for s in summed)
    keep_feat = 1.0 - reset_flag.astype(F32)
    keep_rows = lax.dynamic_slice_in_dim(keep_feat, lax.axis_index("row") * rows_w, rows_w)[:, None]
    keep_cols = lax.dynamic_slice_in_dim(keep_feat, lax.axis_index("grp") * vcols, vcols)[None, :]
    bias_index = (my_number(cube) * bias + jnp.arange(bias, dtype=jnp.int32)) % D
    keeps = (keep_rows, keep_rows, keep_rows, keep_cols, keep_cols, keep_feat[bias_index])
    weights = (w_qkv, w_out, w_fc, w_proj, vectors, fc_bias)
    firsts = (first_qkv, first_out, first_fc, first_proj, first_vectors, first_fc_bias)
    seconds = (second_qkv, second_out, second_fc, second_proj, second_vectors, second_fc_bias)
    updated = [
        adam_update(w, m, v, g, kp) for w, m, v, g, kp in zip(weights, firsts, seconds, grads, keeps)
    ]
    return (
        (hidden, input_grad)
        + grads
        + tuple(u[0] for u in updated)
        + tuple(u[1] for u in updated)
        + tuple(u[2] for u in updated)
    )


def solution(mesh):
    tokens = P(("grp", "row"), None)
    flat = P(("grp", "row"))
    tiles = P("row", "grp")
    six = (tiles, tiles, tiles, tiles, tiles, flat)
    return jax.shard_map(
        body,
        mesh=mesh,
        in_specs=(tokens, tokens) + six * 3 + (tokens, P("grp"), P()),
        out_specs=(tokens, tokens) + six * 4,
        check_vma=False,
    )
```

time: 1260 us -> 685 us (0.54)
  waiting for transfers between devices: 786 us -> 124 us
  Pallas kernels: 0 us -> 444 us
  blocking collectives: 169 us -> 0 us
  matrix products: 138 us -> 0 us
  local copies, waits for them, and re-layouts: 91.8 us -> 28.4 us
  starting transfers between devices: 0.54 us -> 39.2 us
  between operations: 17.8 us -> 5 us
    reduce_scatter x6 -> x0, waiting for transfers between devices: 486 us -> none  [the longest x1 125 us: reduce_row(): lax.psum_scatter(parts[1], 'row', scatter_dimension=0, tiled=True)]
    pallas_call x0 -> x14, Pallas kernels: none -> 444 us  [the longest x1 144 us: assemble_fc(): kernel_call(body, outs, [HB, HB], [pltpu.SemaphoreType.DMA], [HB])]
    all_gather x4 -> x0, waiting for transfers between devices: 175 us -> none  [the longest x1 81.6 us: gather_weights(): lax.all_gather(rows[2], 'grp', axis=1, tiled=True)]
    dot_general x19 -> x0, matrix products: 138 us -> none  [the longest x1 21.2 us: backward_pass(): jnp.einsum('hqk,khd->qhd', d_scores_low, keys, preferred_element_type=jnp...]
    unnamed x16 -> x0, waiting for transfers between devices: 125 us -> none
    ppermute x0 -> x30, waiting for transfers between devices: none -> 124 us  [the longest x24 124 us: swap(): return lax.ppermute(x, BOTH, pairs)]
    all_gather x7 -> x0, blocking collectives: 90.9 us -> none  [the longest x1 26.5 us: gather_weights(): lax.all_gather(rows[5], 'grp', axis=0, tiled=True)]
    psum x1 -> x0, blocking collectives: 39.7 us -> none  [body(): total = lax.psum(jnp.sum(valid.astype(jnp.float32)), ('grp', 'row'))]
  transfers between devices with their start and end apart: 13 -> 30, of which waited for: 11 -> 14; matrix products, arithmetic and copies ran while one was open for 5% -> 7% of each run, Pallas kernels for 0% -> 49%
where the time goes in v1:
time: 685 us; the launch traced here: 675 us
  Pallas kernels  444 us (65%)
  waiting for transfers between devices  124 us (18%)
  starting transfers between devices  39.2 us (6%)
  other arithmetic  34.2 us (5%)
  local copies, waits for them, and re-layouts  28.4 us (4%)
    pallas_call x1, Pallas kernels, assemble_fc(): kernel_call(body, outs, [HB, HB], [pltpu.SemaphoreType.DMA], [HB])  144 us
    pallas_call x1, Pallas kernels, assemble_proj(): kernel_call(body, outs, [HB, HB], [pltpu.SemaphoreType.DMA], [HB])  144 us
    ppermute x24, waiting for transfers between devices, swap(): return lax.ppermute(x, BOTH, pairs)  124 us
    pallas_call x2, Pallas kernels, attention_backward_call(): kernel_call(body, outs, [SM] + [VM] * 9, scratch)  36.1 us
    ppermute x24, starting transfers between devices, swap(): return lax.ppermute(x, BOTH, pairs)  34.9 us
    pallas_call x2, Pallas kernels, ffn_forward_call(): return kernel_call(ffn_forward, outs, [VM] * 5)(h_mid, wfc, wpt, vec, fb)  27.1 us
    pallas_call x2, Pallas kernels, ffn_backward_call(): kernel_call(ffn_backward, outs, [VM] * 6, [pltpu.VMEM((t, D), F32)])  25.6 us
    pallas_call x2, Pallas kernels, attention_forward_call(): kernel_call(body, outs, [SM, VM, VM, VM, VM], [pltpu.VMEM((t, t), F32)])  25.6 us
  transfers between devices with their start and end apart: 30, of which 14 were waited for; matrix products, arithmetic and copies ran while one was open for 7% of the time, Pallas kernels for 49%

profile of v1, /device:TPU:0, one launch (start us, length us, event | category | flops | bytes accessed | tf_op | source)
XLA Modules:
  0.0 675.3 jit_solution(12871513635695812005)
XLA Ops:
  8.0 4.0 collective-permute-start
  12.1 11.5 %collective-permute-done = bf16[1,208,384]{2,1,0:T(8,128)(2,1)S(1)} collective-permute-done((bf16[1,208,384]{2,1,0:T(8,128)(2,1)S(1)}, bf16[1,208,384]{2,1,0:T(8,128)(2,1)S(1)}, u32[]{:S(2)}, u32[]{:S(2)}) %collective-permute-start) | collective-permute-done | bytes 159776 | tf_op jit(solution)/shard_map/ppermute | solution.py:285
  28.1 6.7 collective-permute-done.10
  35.8 3.7 collective-permute-start.11
  41.9 6.6 collective-permute-done.11
  53.3 11.5 %collective-permute-done.12 = bf16[4,96,768]{2,1,0:T(8,128)(2,1)S(1)} collective-permute-done((bf16[4,96,768]{2,1,0:T(8,128)(2,1)S(1)}, bf16[4,96,768]{2,1,0:T(8,128)(2,1)S(1)}, u32[]{:S(2)}, u32[]{:S(2)}) %collective-permute-start.12) | collective-permute-done | bytes 589856 | tf_op jit(solution)/shard_map/ppermute | solution.py:285
  66.5 10.9 %collective-permute-done.7 = bf16[4,192,384]{2,1,0:T(8,128)(2,1)S(1)} collective-permute-done((bf16[4,192,384]{2,1,0:T(8,128)(2,1)S(1)}, bf16[4,192,384]{2,1,0:T(8,128)(2,1)S(1)}, u32[]{:S(2)}, u32[]{:S(2)}) %collective-permute-start.7) | collective-permute-done | bytes 589856 | tf_op jit(solution)/shard_map/ppermute | solution.py:285
  84.5 4.5 collective-permute-done.13
  91.1 10.5 %collective-permute-done.8 = bf16[8,192,384]{2,1,0:T(8,128)(2,1)S(1)} collective-permute-done((bf16[8,192,384]{2,1,0:T(8,128)(2,1)S(1)}, bf16[8,192,384]{2,1,0:T(8,128)(2,1)S(1)}, u32[]{:S(2)}, u32[]{:S(2)}) %collective-permute-start.8) | collective-permute-done | bytes 1179680 | tf_op jit(solution)/shard_map/ppermute | solution.py:285
  107.1 144.0 %shard_map.425.wpt = bf16[768,3072]{1,0:T(8,128)(2,1)} custom-call(bf16[16,96,768]{2,1,0:T(8,128)(2,1)} %copy-done.7, bf16[16,96,768]{2,1,0:T(8,128)(2,1)} %collective-permute-done.14.other), custom_call_target="tpu_custom_call" | custom-call | tf_op jit(solution)/shard_map/pallas_call | solution.py:385
  251.2 144.1 %shard_map.424.wfc = bf16[768,3072]{1,0:T(8,128)(2,1)} custom-call(bf16[16,192,384]{2,1,0:T(8,128)(2,1)} %constant_dynamic-update-slice_fusion.5.held, bf16[16,192,384]{2,1,0:T(8,128)(2,1)} %collective-permute-done.9.other), custom_call_target="tpu_custom_call" | custom-call | tf_op jit(solution)/shard_map/pallas_call | solution.py:369
  395.3 6.5 shard_map.422
  401.8 12.8 %shard_map.423 = (bf16[512,768]{1,0:T(8,128)(2,1)}, bf16[512,2304]{1,0:T(8,128)(2,1)}, f32[512,128]{1,0:T(8,128)}, bf16[512,768]{1,0:T(8,128)(2,1)}, f32[512,768]{1,0:T(8,128)}) custom-call(s32[1,8]{1,0:T(1,128)} %ends.7, bf16[512,768]{1,0:T(8,128)(2,1)} %h.3, bf16[768,2304]{1,0:T(8,128)(2,1)} %get-tuple-element.66.wqkv, ...), custom_call_target="tpu_custom_call" | custom-call | tf_op jit(solution)/shard_map/pallas_call | solution.py:229
  414.5 13.6 %shard_map.426 = (bf16[512,768]{1,0:T(8,128)(2,1)}, bf16[512,3072]{1,0:T(8,128)(2,1)}, bf16[512,3072]{1,0:T(8,128)(2,1)}, f32[512,768]{1,0:T(8,128)}) custom-call(f32[512,768]{1,0:T(8,128)} %get-tuple-element.69.h_mid, bf16[768,3072]{1,0:T(8,128)(2,1)} %shard_map.424.wfc, bf16[768,3072]{1,0:T(8,128)(2,1)} %shard_map.425.wpt, ...), custom_call_target="tpu_custom_call" | custom-call | tf_op jit(solution)/shard_map/pallas_call | solution.py:237
  428.1 12.8 %shard_map.427 = (bf16[512,768]{1,0:T(8,128)(2,1)}, bf16[512,2304]{1,0:T(8,128)(2,1)}, f32[512,128]{1,0:T(8,128)}, bf16[512,768]{1,0:T(8,128)(2,1)}, f32[512,768]{1,0:T(8,128)}) custom-call(s32[1,8]{1,0:T(1,128)} %ends.7, f32[512,768]{1,0:T(8,128)} %get-tuple-element.71.h, bf16[768,2304]{1,0:T(8,128)(2,1)} %get-tuple-element.66.wqkv, ...), custom_call_target="tpu_custom_call" | custom-call | tf_op jit(solution)/shard_map/pallas_call | solution.py:229
  440.9 13.5 %shard_map.428 = (bf16[512,768]{1,0:T(8,128)(2,1)}, bf16[512,3072]{1,0:T(8,128)(2,1)}, bf16[512,3072]{1,0:T(8,128)(2,1)}, f32[512,768]{1,0:T(8,128)}) custom-call(f32[512,768]{1,0:T(8,128)} %get-tuple-element.72.h_mid, bf16[768,3072]{1,0:T(8,128)(2,1)} %shard_map.424.wfc, bf16[768,3072]{1,0:T(8,128)(2,1)} %shard_map.425.wpt, ...), custom_call_target="tpu_custom_call" | custom-call | tf_op jit(solution)/shard_map/pallas_call | solution.py:237
  454.4 12.8 %shard_map.429 = (bf16[512,768]{1,0:T(8,128)(2,1)}, bf16[512,3072]{1,0:T(8,128)(2,1)}, f32[1,3072]{1,0:T(1,128)}, f32[512,768]{1,0:T(8,128)}, bf16[512,768]{1,0:T(8,128)(2,1)}, /*index=5*/f32[8,768]{1,0:T(8,128)}) custom-call(f32[512,768]{1,0:T(8,128)} %fusion.1.dy, f32[512,768]{1,0:T(8,128)} %get-tuple-element.72.h_mid, ...), custom_call_target="tpu_custom_call" | custom-call | tf_op jit(solution)/shard_map/pallas_call | solution.py:250
  467.3 18.3 %shard_map.430 = (bf16[512,2304]{1,0:T(8,128)(2,1)}, f32[512,768]{1,0:T(8,128)}, f32[8,768]{1,0:T(8,128)}) custom-call(s32[1,8]{1,0:T(1,128)} %ends.7, f32[512,768]{1,0:T(8,128)} %get-tuple-element.75.dh_mid, bf16[512,768]{1,0:T(8,128)(2,1)} %get-tuple-element.76.dh_low.dh1, f32[512,768]{1,0:T(8,128)} %get-tuple-element.71.h, ...), custom_call_target="tpu_custom_call" | custom-call | tf_op jit(solution)/shard_map/pallas_call | solution.py:268
  488.6 12.8 %shard_map.431 = (bf16[512,768]{1,0:T(8,128)(2,1)}, bf16[512,3072]{1,0:T(8,128)(2,1)}, f32[1,3072]{1,0:T(1,128)}, f32[512,768]{1,0:T(8,128)}, bf16[512,768]{1,0:T(8,128)(2,1)}, /*index=5*/f32[8,768]{1,0:T(8,128)}) custom-call(f32[512,768]{1,0:T(8,128)} %get-tuple-element.131.dy, f32[512,768]{1,0:T(8,128)} %get-tuple-element.69.h_mid, ...), custom_call_target="tpu_custom_call" | custom-call | tf_op jit(solution)/shard_map/pallas_call | solution.py:250
  501.3 12.4 %shard_map.434 = bf16[32,192,384]{2,1,0:T(8,128)(2,1)} custom-call(bf16[512,768]{1,0:T(8,128)(2,1)} %get-tuple-element.99.c1, bf16[512,768]{1,0:T(8,128)(2,1)} %get-tuple-element.100.c0, bf16[512,3072]{1,0:T(8,128)(2,1)} %get-tuple-element.101.df1, bf16[512,3072]{1,0:T(8,128)(2,1)} %get-tuple-element.102.df0), custom_call_target="tpu_custom_call" | custom-call | tf_op jit(solution)/shard_map/pallas_call | solution.py:465
  517.0 10.8 %shard_map.435 = bf16[32,96,768]{2,1,0:T(8,128)(2,1)} custom-call(bf16[512,768]{1,0:T(8,128)(2,1)} %get-tuple-element.103.dy1, bf16[512,768]{1,0:T(8,128)(2,1)} %get-tuple-element.130.dy0, bf16[512,3072]{1,0:T(8,128)(2,1)} %get-tuple-element.104.g1, bf16[512,3072]{1,0:T(8,128)(2,1)} %get-tuple-element.105.g0), custom_call_target="tpu_custom_call" | custom-call | tf_op jit(solution)/shard_map/pallas_call | solution.py:487
  532.1 17.9 %shard_map.432 = (bf16[512,2304]{1,0:T(8,128)(2,1)}, f32[512,768]{1,0:T(8,128)}, f32[8,768]{1,0:T(8,128)}) custom-call(s32[1,8]{1,0:T(1,128)} %ends.7, f32[512,768]{1,0:T(8,128)} %get-tuple-element.82.dh_mid, bf16[512,768]{1,0:T(8,128)(2,1)} %get-tuple-element.83.dh_low.dh0, bf16[512,768]{1,0:T(8,128)(2,1)} %h.3, bf16[512,2304]{1,0:T(8,128)(2,1)} %get-tuple-element.84.qkv, ...), custom_call_target="tpu_custom_call" | custom-call | tf_op jit(solution)/shard_map/pallas_call | solution.py:268
  551.4 12.2 %shard_map.433 = bf16[32,208,384]{2,1,0:T(8,128)(2,1)} custom-call(bf16[512,768]{1,0:T(8,128)(2,1)} %get-tuple-element.88.a1, bf16[512,768]{1,0:T(8,128)(2,1)} %get-tuple-element.89.a0, bf16[512,2304]{1,0:T(8,128)(2,1)} %get-tuple-element.90.dq1, bf16[512,2304]{1,0:T(8,128)(2,1)} %get-tuple-element.91.dq0, bf16[512,768]{1,0:T(8,128)(2,1)} %get-tuple-element.79.mixed.m1, ...), custom_call_target="tpu_custom_call" | custom-call | tf_op jit(solution)/shard_map/pallas_call | solution.py:539
  563.6 3.6 slice.147
  583.8 5.2 collective-permute-done.21
  590.9 17.1 %collective-permute-done.26 = bf16[8,96,768]{2,1,0:T(8,128)(2,1)} collective-permute-done((bf16[8,96,768]{2,1,0:T(8,128)(2,1)}, bf16[8,96,768]{2,1,0:T(8,128)(2,1)}, u32[]{:S(2)}, u32[]{:S(2)}) %collective-permute-start.26) | collective-permute-done | bytes 1179680 | tf_op jit(solution)/shard_map/ppermute | solution.py:285
  609.6 18.4 %collective-permute-done.16 = bf16[8,208,384]{2,1,0:T(8,128)(2,1)} collective-permute-done((bf16[8,208,384]{2,1,0:T(8,128)(2,1)}, bf16[8,208,384]{2,1,0:T(8,128)(2,1)}, u32[]{:S(2)}, u32[]{:S(2)}) %collective-permute-start.16) | collective-permute-done | bytes 1277984 | tf_op jit(solution)/shard_map/ppermute | solution.py:285
  634.3 5.3 collective-permute-done.23
  639.7 4.0 collective-permute-start.24
  644.6 4.5 collective-permute-done.28
  653.2 5.6 collective-permute-done.18
  663.1 5.9 collective-permute-done.19
  (190 shorter events, 86.6 us)
Async XLA Ops:
  0.7 40.6 %copy-start.5 = (bf16[192,384]{1,0:T(8,128)(2,1)S(1)}, bf16[192,384]{1,0:T(8,128)(2,1)}, u32[]{:S(2)}) copy-start(bf16[192,384]{1,0:T(8,128)(2,1)} %param.27) | copy-start | bytes 442372
  0.7 47.8 %copy-start.4 = (bf16[768,96]{0,1:T(8,128)(2,1)S(1)}, bf16[768,96]{0,1:T(8,128)(2,1)}, u32[]{:S(2)}) copy-start(bf16[768,96]{0,1:T(8,128)(2,1)} %param.28) | copy-start | bytes 442372
  8.0 15.6 %collective-permute-start = (bf16[1,208,384]{2,1,0:T(8,128)(2,1)S(1)}, bf16[1,208,384]{2,1,0:T(8,128)(2,1)S(1)}, u32[]{:S(2)}, u32[]{:S(2)}) collective-permute-start(bf16[1,208,384]{2,1,0:T(8,128)(2,1)S(1)} %get-tuple-element.133), channel_id=1, source_target_pairs={{0,16},{1,17},{2,18},{3,19},{4,20},{5,21},{6,22},{7,23},{8,24},{9,... | collective-permute-start | bytes 479240 | tf_op jit(solution)/shard_map/ppermute | solution.py:285
  12.0 15.0 %collective-permute-start.5 = (bf16[1,192,384]{2,1,0:T(8,128)(2,1)}, bf16[1,192,384]{2,1,0:T(8,128)(2,1)S(1)}, u32[]{:S(2)}, u32[]{:S(2)}) collective-permute-start(bf16[1,192,384]{2,1,0:T(8,128)(2,1)} %bitcast.41), channel_id=1, source_target_pairs={{0,16},{1,17},{2,18},{3,19},{4,20},{5,21},{6,22},{7,23},{8,24},{9,... | collective-permute-start | bytes 442376 | tf_op jit(solution)/shard_map/ppermute | solution.py:285
  23.6 16.0 %collective-permute-start.1 = (bf16[2,208,384]{2,1,0:T(8,128)(2,1)S(1)}, bf16[2,208,384]{2,1,0:T(8,128)(2,1)S(1)}, u32[]{:S(2)}, u32[]{:S(2)}) collective-permute-start(bf16[2,208,384]{2,1,0:T(8,128)(2,1)S(1)} %pad_maximum_fusion.6), channel_id=1, source_target_pairs={{0,8},{1,9},{2,10},{3,11},{4,12},{5,13},{6,14},{7,15},{8,0},{9,1},... | collective-permute-start | bytes 958472 | tf_op jit(solution)/shard_map/ppermute | solution.py:285
  23.7 11.2 %collective-permute-start.10 = (bf16[1,96,768]{2,1,0:T(8,128)(2,1)}, bf16[1,96,768]{2,1,0:T(8,128)(2,1)S(1)}, u32[]{:S(2)}, u32[]{:S(2)}) collective-permute-start(bf16[1,96,768]{2,1,0:T(8,128)(2,1)} %bitcast.37), channel_id=1, source_target_pairs={{0,16},{1,17},{2,18},{3,19},{4,20},{5,21},{6,22},{7,23},{8,24},{9,... | collective-permute-start | bytes 442376 | tf_op jit(solution)/shard_map/ppermute | solution.py:285
  28.0 22.3 %collective-permute-start.6 = (bf16[2,192,384]{2,1,0:T(8,128)(2,1)S(1)}, bf16[2,192,384]{2,1,0:T(8,128)(2,1)S(1)}, u32[]{:S(2)}, u32[]{:S(2)}) collective-permute-start(bf16[2,192,384]{2,1,0:T(8,128)(2,1)S(1)} %pad_maximum_fusion.7), channel_id=1, source_target_pairs={{0,8},{1,9},{2,10},{3,11},{4,12},{5,13},{6,14},{7,15},{8,0},{9,1},... | collective-permute-start | bytes 884744 | tf_op jit(solution)/shard_map/ppermute | solution.py:285
  35.8 12.7 %collective-permute-start.11 = (bf16[2,96,768]{2,1,0:T(8,128)(2,1)S(1)}, bf16[2,96,768]{2,1,0:T(8,128)(2,1)S(1)}, u32[]{:S(2)}, u32[]{:S(2)}) collective-permute-start(bf16[2,96,768]{2,1,0:T(8,128)(2,1)S(1)} %pad_maximum_fusion.8), channel_id=1, source_target_pairs={{0,8},{1,9},{2,10},{3,11},{4,12},{5,13},{6,14},{7,15},{8,0},{9,1},... | collective-permute-start | bytes 884744 | tf_op jit(solution)/shard_map/ppermute | solution.py:285
  39.6 11.2 %collective-permute-start.2 = (bf16[4,208,384]{2,1,0:T(8,128)(2,1)S(1)}, bf16[4,208,384]{2,1,0:T(8,128)(2,1)S(1)}, u32[]{:S(2)}, u32[]{:S(2)}) collective-permute-start(bf16[4,208,384]{2,1,0:T(8,128)(2,1)S(1)} %pad_maximum_fusion.3), channel_id=1, source_target_pairs={{0,4},{1,3},{2,6},{3,1},{4,0},{5,7},{6,2},{7,5},{8,12},{9,11},{10,... | collective-permute-start | bytes 1916936 | tf_op jit(solution)/shard_map/ppermute | solution.py:285
  48.6 16.2 %collective-permute-start.12 = (bf16[4,96,768]{2,1,0:T(8,128)(2,1)S(1)}, bf16[4,96,768]{2,1,0:T(8,128)(2,1)S(1)}, u32[]{:S(2)}, u32[]{:S(2)}) collective-permute-start(bf16[4,96,768]{2,1,0:T(8,128)(2,1)S(1)} %pad_maximum_fusion.5), channel_id=1, source_target_pairs={{0,4},{1,3},{2,6},{3,1},{4,0},{5,7},{6,2},{7,5},{8,12},{9,11},{10,... | collective-permute-start | bytes 1769480 | tf_op jit(solution)/shard_map/ppermute | solution.py:285
  50.3 27.1 %collective-permute-start.7 = (bf16[4,192,384]{2,1,0:T(8,128)(2,1)S(1)}, bf16[4,192,384]{2,1,0:T(8,128)(2,1)S(1)}, u32[]{:S(2)}, u32[]{:S(2)}) collective-permute-start(bf16[4,192,384]{2,1,0:T(8,128)(2,1)S(1)} %pad_maximum_fusion.4), channel_id=1, source_target_pairs={{0,4},{1,3},{2,6},{3,1},{4,0},{5,7},{6,2},{7,5},{8,12},{9,11},{10,... | collective-permute-start | bytes 1769480 | tf_op jit(solution)/shard_map/ppermute | solution.py:285
  51.0 32.3 %collective-permute-start.3 = (bf16[8,208,384]{2,1,0:T(8,128)(2,1)S(1)}, bf16[8,208,384]{2,1,0:T(8,128)(2,1)S(1)}, u32[]{:S(2)}, u32[]{:S(2)}) collective-permute-start(bf16[8,208,384]{2,1,0:T(8,128)(2,1)S(1)} %pad_maximum_fusion), channel_id=1, source_target_pairs={{0,2},{1,5},{2,0},{3,7},{4,6},{5,1},{6,4},{7,3},{8,10},{9,13},{10,... | collective-permute-start | bytes 3833864 | tf_op jit(solution)/shard_map/ppermute | solution.py:285
  64.9 24.0 %collective-permute-start.13 = (bf16[8,96,768]{2,1,0:T(8,128)(2,1)S(1)}, bf16[8,96,768]{2,1,0:T(8,128)(2,1)S(1)}, u32[]{:S(2)}, u32[]{:S(2)}) collective-permute-start(bf16[8,96,768]{2,1,0:T(8,128)(2,1)S(1)} %pad_maximum_fusion.2), channel_id=1, source_target_pairs={{0,2},{1,5},{2,0},{3,7},{4,6},{5,1},{6,4},{7,3},{8,10},{9,13},{10,... | collective-permute-start | bytes 3538952 | tf_op jit(solution)/shard_map/ppermute | solution.py:285
  77.6 24.0 %collective-permute-start.8 = (bf16[8,192,384]{2,1,0:T(8,128)(2,1)S(1)}, bf16[8,192,384]{2,1,0:T(8,128)(2,1)S(1)}, u32[]{:S(2)}, u32[]{:S(2)}) collective-permute-start(bf16[8,192,384]{2,1,0:T(8,128)(2,1)S(1)} %pad_maximum_fusion.1), channel_id=1, source_target_pairs={{0,2},{1,5},{2,0},{3,7},{4,6},{5,1},{6,4},{7,3},{8,10},{9,13},{10,... | collective-permute-start | bytes 3538952 | tf_op jit(solution)/shard_map/ppermute | solution.py:285
  84.5 310.8 %collective-permute-start.4 = (bf16[16,208,384]{2,1,0:T(8,128)(2,1)}, bf16[16,208,384]{2,1,0:T(8,128)(2,1)}, u32[]{:S(2)}, u32[]{:S(2)}) collective-permute-start(bf16[16,208,384]{2,1,0:T(8,128)(2,1)} %constant_dynamic-update-slice_fusion.held), channel_id=1, source_target_pairs={{0,1},{1,0},{2,3},{3,2},{4,5},{5,4},{6,7},{7,6},{8,9},{9,8},{10,11... | collective-permute-start | bytes 7667720 | tf_op jit(solution)/shard_map/ppermute | solution.py:288
  89.0 18.1 %collective-permute-start.14 = (bf16[16,96,768]{2,1,0:T(8,128)(2,1)S(1)}, bf16[16,96,768]{2,1,0:T(8,128)(2,1)}, u32[]{:S(2)}, u32[]{:S(2)}) collective-permute-start(bf16[16,96,768]{2,1,0:T(8,128)(2,1)S(1)} %constant_dynamic-update-slice_fusion.10.held), channel_id=1, source_target_pairs={{0,1},{1,0},{2,3},{3,2},{4,5},{5,4},{6,7},{7,6},{8,9},{9,8},{10,11... | collective-permute-start | bytes 7077896 | tf_op jit(solution)/shard_map/ppermute | solution.py:288
  102.7 148.5 %collective-permute-start.9 = (bf16[16,192,384]{2,1,0:T(8,128)(2,1)}, bf16[16,192,384]{2,1,0:T(8,128)(2,1)}, u32[]{:S(2)}, u32[]{:S(2)}) collective-permute-start(bf16[16,192,384]{2,1,0:T(8,128)(2,1)} %constant_dynamic-update-slice_fusion.5.held), channel_id=1, source_target_pairs={{0,1},{1,0},{2,3},{3,2},{4,5},{5,4},{6,7},{7,6},{8,9},{9,8},{10,11... | collective-permute-start | bytes 7077896 | tf_op jit(solution)/shard_map/ppermute | solution.py:288
  517.0 50.2 %collective-permute-start.20 = (bf16[16,192,384]{2,1,0:T(8,128)(2,1)}, bf16[16,192,384]{2,1,0:T(8,128)(2,1)}, u32[]{:S(2)}, u32[]{:S(2)}) collective-permute-start(bf16[16,192,384]{2,1,0:T(8,128)(2,1)} %slice.159), channel_id=1, source_target_pairs={{0,1},{1,0},{2,3},{3,2},{4,5},{5,4},{6,7},{7,6},{8,9},{9,8},{10,11... | collective-permute-start | bytes 7077896 | tf_op jit(solution)/shard_map/ppermute | solution.py:288
  531.0 42.7 %collective-permute-start.25 = (bf16[16,96,768]{2,1,0:T(8,128)(2,1)}, bf16[16,96,768]{2,1,0:T(8,128)(2,1)}, u32[]{:S(2)}, u32[]{:S(2)}) collective-permute-start(bf16[16,96,768]{2,1,0:T(8,128)(2,1)} %slice.169), channel_id=1, source_target_pairs={{0,1},{1,0},{2,3},{3,2},{4,5},{5,4},{6,7},{7,6},{8,9},{9,8},{10,11... | collective-permute-start | bytes 7077896 | tf_op jit(solution)/shard_map/ppermute | solution.py:288
  567.2 10.6 %collective-permute-start.15 = (bf16[16,208,384]{2,1,0:T(8,128)(2,1)}, bf16[16,208,384]{2,1,0:T(8,128)(2,1)}, u32[]{:S(2)}, u32[]{:S(2)}) collective-permute-start(bf16[16,208,384]{2,1,0:T(8,128)(2,1)} %slice.147), channel_id=1, source_target_pairs={{0,1},{1,0},{2,3},{3,2},{4,5},{5,4},{6,7},{7,6},{8,9},{9,8},{10,11... | collective-permute-start | bytes 7667720 | tf_op jit(solution)/shard_map/ppermute | solution.py:288
  572.5 16.5 %collective-permute-start.21 = (bf16[8,192,384]{2,1,0:T(8,128)(2,1)}, bf16[8,192,384]{2,1,0:T(8,128)(2,1)}, u32[]{:S(2)}, u32[]{:S(2)}) collective-permute-start(bf16[8,192,384]{2,1,0:T(8,128)(2,1)} %slice.161), channel_id=1, source_target_pairs={{0,2},{1,5},{2,0},{3,7},{4,6},{5,1},{6,4},{7,3},{8,10},{9,13},{10,... | collective-permute-start | bytes 3538952 | tf_op jit(solution)/shard_map/ppermute | solution.py:285
  576.9 31.1 %collective-permute-start.26 = (bf16[8,96,768]{2,1,0:T(8,128)(2,1)}, bf16[8,96,768]{2,1,0:T(8,128)(2,1)}, u32[]{:S(2)}, u32[]{:S(2)}) collective-permute-start(bf16[8,96,768]{2,1,0:T(8,128)(2,1)} %slice.171), channel_id=1, source_target_pairs={{0,2},{1,5},{2,0},{3,7},{4,6},{5,1},{6,4},{7,3},{8,10},{9,13},{10,... | collective-permute-start | bytes 3538952 | tf_op jit(solution)/shard_map/ppermute | solution.py:285
  581.4 46.6 %collective-permute-start.16 = (bf16[8,208,384]{2,1,0:T(8,128)(2,1)}, bf16[8,208,384]{2,1,0:T(8,128)(2,1)}, u32[]{:S(2)}, u32[]{:S(2)}) collective-permute-start(bf16[8,208,384]{2,1,0:T(8,128)(2,1)} %slice.149), channel_id=1, source_target_pairs={{0,2},{1,5},{2,0},{3,7},{4,6},{5,1},{6,4},{7,3},{8,10},{9,13},{10,... | collective-permute-start | bytes 3833864 | tf_op jit(solution)/shard_map/ppermute | solution.py:285
  590.9 38.8 %collective-permute-start.22 = (bf16[4,192,384]{2,1,0:T(8,128)(2,1)S(1)}, bf16[4,192,384]{2,1,0:T(8,128)(2,1)S(1)}, u32[]{:S(2)}, u32[]{:S(2)}) collective-permute-start(bf16[4,192,384]{2,1,0:T(8,128)(2,1)S(1)} %slice.163), channel_id=1, source_target_pairs={{0,4},{1,3},{2,6},{3,1},{4,0},{5,7},{6,2},{7,5},{8,12},{9,11},{10,... | collective-permute-start | bytes 1769480 | tf_op jit(solution)/shard_map/ppermute | solution.py:285
  609.5 24.4 %collective-permute-start.27 = (bf16[4,96,768]{2,1,0:T(8,128)(2,1)S(1)}, bf16[4,96,768]{2,1,0:T(8,128)(2,1)S(1)}, u32[]{:S(2)}, u32[]{:S(2)}) collective-permute-start(bf16[4,96,768]{2,1,0:T(8,128)(2,1)S(1)} %slice.173), channel_id=1, source_target_pairs={{0,4},{1,3},{2,6},{3,1},{4,0},{5,7},{6,2},{7,5},{8,12},{9,11},{10,... | collective-permute-start | bytes 1769480 | tf_op jit(solution)/shard_map/ppermute | solution.py:285
  629.6 14.1 %collective-permute-start.17 = (bf16[4,208,384]{2,1,0:T(8,128)(2,1)S(1)}, bf16[4,208,384]{2,1,0:T(8,128)(2,1)S(1)}, u32[]{:S(2)}, u32[]{:S(2)}) collective-permute-start(bf16[4,208,384]{2,1,0:T(8,128)(2,1)S(1)} %slice.151), channel_id=1, source_target_pairs={{0,4},{1,3},{2,6},{3,1},{4,0},{5,7},{6,2},{7,5},{8,12},{9,11},{10,... | collective-permute-start | bytes 1916936 | tf_op jit(solution)/shard_map/ppermute | solution.py:285
  629.8 9.9 %collective-permute-start.23 = (bf16[2,192,384]{2,1,0:T(8,128)(2,1)S(1)}, bf16[2,192,384]{2,1,0:T(8,128)(2,1)S(1)}, u32[]{:S(2)}, u32[]{:S(2)}) collective-permute-start(bf16[2,192,384]{2,1,0:T(8,128)(2,1)S(1)} %slice.165), channel_id=1, source_target_pairs={{0,8},{1,9},{2,10},{3,11},{4,12},{5,13},{6,14},{7,15},{8,0},{9,1},... | collective-permute-start | bytes 884744 | tf_op jit(solution)/shard_map/ppermute | solution.py:285
  634.0 15.1 %collective-permute-start.28 = (bf16[2,96,768]{2,1,0:T(8,128)(2,1)S(1)}, bf16[2,96,768]{2,1,0:T(8,128)(2,1)S(1)}, u32[]{:S(2)}, u32[]{:S(2)}) collective-permute-start(bf16[2,96,768]{2,1,0:T(8,128)(2,1)S(1)} %slice.175), channel_id=1, source_target_pairs={{0,8},{1,9},{2,10},{3,11},{4,12},{5,13},{6,14},{7,15},{8,0},{9,1},... | collective-permute-start | bytes 884744 | tf_op jit(solution)/shard_map/ppermute | solution.py:285
  639.7 11.6 %collective-permute-start.24 = (bf16[1,192,384]{2,1,0:T(8,128)(2,1)S(1)}, bf16[1,192,384]{2,1,0:T(8,128)(2,1)S(1)}, u32[]{:S(2)}, u32[]{:S(2)}) collective-permute-start(bf16[1,192,384]{2,1,0:T(8,128)(2,1)S(1)} %slice.167), channel_id=1, source_target_pairs={{0,16},{1,17},{2,18},{3,19},{4,20},{5,21},{6,22},{7,23},{8,24},{9,... | collective-permute-start | bytes 442376 | tf_op jit(solution)/shard_map/ppermute | solution.py:285
  643.8 15.0 %collective-permute-start.18 = (bf16[2,208,384]{2,1,0:T(8,128)(2,1)S(1)}, bf16[2,208,384]{2,1,0:T(8,128)(2,1)S(1)}, u32[]{:S(2)}, u32[]{:S(2)}) collective-permute-start(bf16[2,208,384]{2,1,0:T(8,128)(2,1)S(1)} %slice.153), channel_id=1, source_target_pairs={{0,8},{1,9},{2,10},{3,11},{4,12},{5,13},{6,14},{7,15},{8,0},{9,1},... | collective-permute-start | bytes 958472 | tf_op jit(solution)/shard_map/ppermute | solution.py:285
  649.2 12.1 %collective-permute-start.29 = (bf16[1,96,768]{2,1,0:T(8,128)(2,1)S(1)}, bf16[1,96,768]{2,1,0:T(8,128)(2,1)S(1)}, u32[]{:S(2)}, u32[]{:S(2)}) collective-permute-start(bf16[1,96,768]{2,1,0:T(8,128)(2,1)S(1)} %slice.177), channel_id=1, source_target_pairs={{0,16},{1,17},{2,18},{3,19},{4,20},{5,21},{6,22},{7,23},{8,24},{9,... | collective-permute-start | bytes 442376 | tf_op jit(solution)/shard_map/ppermute | solution.py:285
  658.9 10.2 %collective-permute-start.19 = (bf16[1,208,384]{2,1,0:T(8,128)(2,1)S(1)}, bf16[1,208,384]{2,1,0:T(8,128)(2,1)S(1)}, u32[]{:S(2)}, u32[]{:S(2)}) collective-permute-start(bf16[1,208,384]{2,1,0:T(8,128)(2,1)S(1)} %slice.155), channel_id=1, source_target_pairs={{0,16},{1,17},{2,18},{3,19},{4,20},{5,21},{6,22},{7,23},{8,24},{9,... | collective-permute-start | bytes 479240 | tf_op jit(solution)/shard_map/ppermute | solution.py:285
  (33 other events, 428.1 us)
